TPU v7x, 32 devices: a whole 2x2x4 slice. The times are simulated.
32 devices in a mesh: dp: 2 (over x), pipe: 4 (over y, core), tensor: 4 (over z).
Axes of the slice: x: 2, y: 2, z: 4, core: 2. Of those that a mesh axis runs over, the one named last changes fastest.
Arguments:
- grad_out: bfloat16 [8, 128, 4096], P(None, 'dp', 'tensor'), may hold values from -6 to 6
- activations: bfloat16 [4, 3, 8, 128, 4096], P('pipe', None, None, 'dp', 'tensor'), may hold values from -6 to 6
- mixing: bfloat16 [4, 3, 32, 128, 128], P('pipe', None, 'tensor'), may hold values from -0.1875 to 0.1875
- proj_tiles: bfloat16 [4, 3, 8, 128, 128], P('pipe'), may hold values from -0.1875 to 0.1875
- proj_blocks: int32 [4, 3, 8], P('pipe'), may hold values from 0 to 31, all different within a row
- section_sizes: int32 [4], replicated, may hold values from 1 to 3, 8 in all
Outputs:
- segment_grads: bfloat16 [4, 8, 128, 4096], P('pipe', None, 'dp', 'tensor')
- sketches: float32 [4, 3, 8, 4096], P('pipe')
Inputs may be any that keep to these rules, and one draw needn't show every extreme that they name: `section_sizes`: each segment holds 1 to 3 layers, 8 in all, some segment exactly 3. `proj_blocks`: the 8 blocks of one slot are distinct.
All inputs are finite; a program needn't handle non-finite values.
Results may differ from a plain program's by a relative error of at most 0.0074.
Values may be sent and summed in bfloat16 or wider, within the bound.
No kernel may reach another device: no remote copies, remote signals or barrier semaphores. Data moves between devices by JAX's collectives and lax.ppermute only.
A program may use at most 64 MiB of HBM per device.

v0:
```python
import functools
import math

import jax
import jax.numpy as jnp
from jax import lax
from jax.experimental import pallas as pl
from jax.experimental.pallas import tpu as pltpu
from jax.sharding import PartitionSpec as P

F32 = jnp.float32
BF16 = jnp.bfloat16
VMEM = pl.BlockSpec(memory_space=pltpu.VMEM)
HBM = pl.BlockSpec(memory_space=pltpu.HBM)
PARAMS = pltpu.CompilerParams(vmem_limit_bytes=16 * 1024 * 1024)
NN = (((1,), (0,)), ((), ()))
NT = (((1,), (1,)), ((), ()))
TN = (((0,), (0,)), ((), ()))
FLAG = (8, 128)
LIGHT = 1000
WORK = (3000, 1000, 6000, 1000, 10000, 6000, 10000, 6000, 10000, 3000, 1, 10000, 2000, 10000, 300, 6000, 1, 300, 1, 10000, 2000, 10000, 3000, 2000, 3000, 1)


def mm(a, b, dims=NN):
    return lax.dot_general(a, b, dims, preferred_element_type=F32)


def silu_slope(value):
    sig = 0.5 + 0.5 * jnp.tanh(0.5 * value)
    return sig * (1.0 + value * (1.0 - sig))


def left_lanes(shape, rank):
    return lax.broadcasted_iota(jnp.int32, shape, len(shape) - 1) < rank


def head_lanes(h, head_size):
    return slice(h * head_size, (h + 1) * head_size)


def live_slots(info):
    return jnp.max(info[...]).astype(jnp.int32)


def here(pair):
    section = lax.axis_index("pipe")
    return section // 2 == pair, section % 2 == 1


def slopes_of(k, at, acts, mix_act, slopes, part=None):
    chunk, tokens, width = slopes.shape[1:]
    heads, head_size = mix_act.shape[1], mix_act.shape[2]
    rows = chunk * tokens
    total = 0.0
    for h in range(heads):
        act = acts[k, at : at + chunk, :, head_lanes(h, head_size)].reshape(rows, head_size)
        if part is None:
            pre = mm(act, mix_act[k, h, :, :head_size])
        else:
            both = mm(act, mix_act[k, h])
            total += both[:, head_size:]
            pre = both[:, :head_size]
        slope = silu_slope(pre).astype(slopes.dtype)
        slopes[k, :, :, head_lanes(h, head_size)] = slope.reshape(chunk, tokens, head_size)
    if part is not None:
        part[k] = total.astype(BF16)


def project_of(k, at, chunk, acts, mix_act):
    tokens = acts.shape[2]
    heads, head_size = mix_act.shape[1], mix_act.shape[2]
    total = 0.0
    for h in range(heads):
        act = acts[k, at : at + chunk, :, head_lanes(h, head_size)].reshape(chunk * tokens, head_size)
        total += mm(act, mix_act[k, h, :, head_size:])
    return total


def chain(live, source, slopes, mix_grad, grad, proj):
    chunk, tokens, width = grad.shape
    heads, head_size = mix_grad.shape[1], mix_grad.shape[3]
    rows = chunk * tokens
    grad[...] = source

    def slot(i, _):
        k = live - 1 - i
        old, both = [], []
        for h in range(heads):
            lanes = head_lanes(h, head_size)
            g = grad[:, :, lanes].reshape(rows, head_size).astype(F32)
            delta = (g * slopes[k, :, :, lanes].reshape(rows, head_size).astype(F32)).astype(BF16)
            old.append(g)
            both.append(mm(delta, mix_grad[k, h], NT))
        total = jnp.zeros((rows, proj.shape[2]), F32)
        for h in range(heads):
            lanes = head_lanes(h, head_size)
            grad[:, :, lanes] = (old[h] + both[h][:, :head_size]).astype(BF16).reshape(chunk, tokens, head_size)
            total += both[h][:, head_size:]
        proj[k] = total.astype(BF16)
        return 0

    lax.fori_loop(0, live, slot, 0)


def spread_tiles(k, blocks, tiles, mix_act, mix_grad):
    picks, head_size, both = tiles.shape[1:]
    rank = both // 2
    heads = mix_act.shape[1]
    first_head = lax.axis_index("tensor") * heads
    row = lax.broadcasted_iota(jnp.int32, (both, both), 0)
    col = lax.broadcasted_iota(jnp.int32, (both, both), 1)
    twice = (row == col % rank).astype(BF16)
    order = rank + jnp.where(row < rank // 2, 2 * row, 2 * row - rank + 1)
    split = jnp.logical_and(col == order, row < rank).astype(BF16)
    mix_act[k, :, :, head_size:] = jnp.zeros((heads, head_size, both), BF16)
    mix_grad[k, :, head_size:, :] = jnp.zeros((heads, both, head_size), BF16)
    for j in range(picks):
        own = blocks[k, 0, j] - first_head

        @pl.when(jnp.logical_and(own >= 0, own < heads))
        def _():
            tile = tiles[k, j]
            mix_act[k, own, :, head_size:] = mm(tile, twice).astype(BF16)
            mix_grad[k, own, head_size:, :] = mm(split, tile, NT).astype(BF16)


def first_kernel(
    pair, sizes_in, blocks_in, top, acts, mixing, tiles,
    grad, proj, slopes, part, next_slopes, next_part, acts_v, top_v, mix_act, mix_grad, info,
    sizes, blocks, tiles_v, sems,
):
    slots = acts.shape[0]
    head_size = mixing.shape[2]
    chunk, micro = grad.shape[0], acts.shape[1]
    copies = []

    def load(src, dst):
        copy = pltpu.make_async_copy(src, dst, sems.at[len(copies)])
        copy.start()
        copies.append(copy)
        return copy

    order = range(slots - 1, -1, -1)
    scalars = (load(sizes_in, sizes), load(blocks_in, blocks))
    spread = {k: load(tiles.at[k], tiles_v.at[k]) for k in order}
    need = {
        k: (
            load(mixing.at[k], mix_act.at[k, :, :, pl.ds(0, head_size)]),
            load(acts.at[k, pl.ds(0, chunk)], acts_v.at[k, pl.ds(0, chunk)]),
        )
        for k in order
    }
    first = [load(mixing.at[k], mix_grad.at[k, :, pl.ds(0, head_size), :]) for k in order]
    first.append(load(top.at[pl.ds(0, chunk)], top_v.at[pl.ds(0, chunk)]))
    second = [load(acts.at[k, pl.ds(chunk, chunk)], acts_v.at[k, pl.ds(chunk, chunk)]) for k in order]
    left = micro - 2 * chunk
    rest = [load(acts.at[k, pl.ds(2 * chunk, left)], acts_v.at[k, pl.ds(2 * chunk, left)]) for k in order]
    rest.append(load(top.at[pl.ds(chunk, micro - chunk)], top_v.at[pl.ds(chunk, micro - chunk)]))
    for copy in scalars:
        copy.wait()
    live = sizes[lax.axis_index("pipe")]
    info[...] = jnp.full(info.shape, live.astype(F32))
    for k in order:
        spread[k].wait()
        pl.when(k < live)(functools.partial(spread_tiles, k, blocks, tiles_v, mix_act, mix_grad))
    for k in order:
        for copy in need[k]:
            copy.wait()
        pl.when(k < live)(functools.partial(slopes_of, k, 0, acts_v, mix_act, slopes, part))
    for copy in first + second:
        copy.wait()
    active, odd = here(pair)
    ahead = jnp.logical_and(active, odd)

    @pl.when(ahead)
    def _():
        chain(live, top_v[:chunk], slopes, mix_grad, grad, proj)

    for k in order:
        pl.when(jnp.logical_and(k < live, jnp.logical_not(ahead)))(
            functools.partial(slopes_of, k, chunk, acts_v, mix_act, next_slopes, next_part)
        )
    for copy in rest:
        copy.wait()


def lay(act_part, group, k, one, two):
    left = left_lanes(one.shape, one.shape[1] // 2)
    act_part[group, k] = jnp.where(left, one, two).astype(BF16)


def beside_kernel(pair, info, acts, mix_act, after, first_part, second_part, slopes, act_part, token, part):
    chunk = slopes.shape[1]
    live = live_slots(info)
    active, odd = here(pair)
    ahead = jnp.logical_and(active, odd)
    for k in range(acts.shape[0]):

        @pl.when(jnp.logical_and(k < live, ahead))
        def _():
            rest = project_of(k, chunk, 3 * chunk, acts, mix_act)
            rows = rest.shape[0] // 3
            lay(act_part, 0, k, first_part[k], rest[:rows])
            lay(act_part, 1, k, rest[rows : 2 * rows], rest[2 * rows :])

        @pl.when(jnp.logical_and(k < live, jnp.logical_not(ahead)))
        def _():
            slopes_of(k, 2 * chunk, acts, mix_act, slopes, part)
            lay(act_part, 0, k, first_part[k], second_part[k])
            lay(act_part, 1, k, part[k], project_of(k, 3 * chunk, chunk, acts, mix_act))


def slope_kernel(pair, at, info, acts, mix_act, after, slopes, token):
    live = live_slots(info)
    active, odd = here(pair)
    ahead = jnp.logical_and(active, odd)
    for k in range(acts.shape[0]):
        pl.when(jnp.logical_and(k < live, jnp.logical_not(ahead)))(
            functools.partial(slopes_of, k, at, acts, mix_act, slopes)
        )


def top_kernel(pair, at, has_odd, info, mix_grad, after, even_in, even_slopes, *refs):
    refs = list(refs)
    top, acts, mix_act = (refs.pop(0), refs.pop(0), refs.pop(0)) if has_odd else (None, None, None)
    grad, proj, token = refs[:3]
    slopes = refs[3] if has_odd else None
    active, odd = here(pair)

    @pl.when(jnp.logical_and(active, jnp.logical_not(odd)))
    def _():
        chain(live_slots(info), even_in[...], even_slopes, mix_grad, grad, proj)

    if has_odd:
        chunk = grad.shape[0]

        @pl.when(jnp.logical_and(active, odd))
        def _():
            live = live_slots(info)
            for k in range(acts.shape[0] - 1, -1, -1):
                pl.when(k < live)(functools.partial(slopes_of, k, at * chunk, acts, mix_act, slopes))
            chain(live, top[at * chunk : (at + 1) * chunk], slopes, mix_grad, grad, proj)


def step_kernel(pair, parity, info, mix_grad, after, source, slopes, grad, proj, token):
    active, odd = here(pair)

    @pl.when(jnp.logical_and(active, odd if parity else jnp.logical_not(odd)))
    def _():
        chain(live_slots(info), source[...], slopes, mix_grad, grad, proj)


def widen_kernel(group, chunk, mine, other, after, out, token):
    slots, rows, both = mine.shape[1:]
    rank = both // 2
    batch = lax.broadcasted_iota(jnp.int32, (rows, both), 0) // (rows // chunk)
    left = left_lanes((rows, both), rank)
    for k in range(slots):
        act = mine[group, k].astype(F32) + other[group, k].astype(F32)
        swapped = pltpu.roll(act, rank, 1)
        for i in range(2):
            one = jnp.where(left, swapped, act) if i else jnp.where(left, act, swapped)
            for m in range(chunk):
                out[k, i, :, m * both : (m + 1) * both] = jnp.where(batch == m, one, 0.0).astype(BF16)


def add_kernel(mine, other, after, total, token):
    total[...] = (mine[...].astype(F32) + other[...].astype(F32)).astype(total.dtype)


def sketch_kernel(pairs, scale, info, after, *refs):
    projs = [refs[p * 4 : (p + 1) * 4] for p in range(pairs)]
    acts, out, token = refs[pairs * 4 :]
    slots, rows, both = projs[0][0].shape
    rank = both // 2
    chunk = out.shape[1] // 2
    live = live_slots(info)

    def one(ref, i):
        lower = left_lanes((rank // 2, both), rank)
        for k in range(slots):

            @pl.when(k < live)
            def _():
                full = mm(ref[k], acts[k, i], TN)
                for m in range(chunk):
                    even = full[: rank // 2, m * both : (m + 1) * both]
                    uneven = full[rank // 2 : rank, m * both : (m + 1) * both]
                    out[k, i * chunk + m] = (jnp.where(lower, even, uneven) * scale).astype(BF16)

            @pl.when(k >= live)
            def _():
                out[k, i * chunk : (i + 1) * chunk] = jnp.zeros((chunk, rank // 2, both), BF16)

    for p in range(pairs):
        active, odd = here(pairs - 1 - p)

        @pl.when(jnp.logical_and(active, odd))
        def _():
            for i in range(2):
                one(projs[p][i], i)

        @pl.when(jnp.logical_and(active, jnp.logical_not(odd)))
        def _():
            for i in range(2):
                one(projs[p][2 + i], i)


def collect_kernel(pairs, after, *refs):
    out, token = refs[-2:]
    count = (len(refs) - 2) // (2 * pairs)
    chunk = refs[0].shape[0]
    for p in range(pairs):
        active, odd = here(pairs - 1 - p)
        for parity in (1, 0):

            @pl.when(jnp.logical_and(active, odd if parity else jnp.logical_not(odd)))
            def _():
                for c in range(count):
                    out[c * chunk : (c + 1) * chunk] = refs[(2 * p + 1 - parity) * count + c][...]


def last_kernel(after, *refs):
    out = refs[-1]
    groups = [(refs[i], refs[i + 1]) for i in range(0, len(refs) - 1, 2)]
    slots, micro, parts, lanes = groups[0][0].shape
    for k in range(slots):
        total = jnp.concatenate([mine[k].astype(F32) + other[k].astype(F32) for mine, other in groups])
        total = jnp.swapaxes(total, 0, 1)
        for i in range(parts):
            out[k, :, i * lanes : (i + 1) * lanes] = total[i]


def swaps(axes):
    for axis in axes:
        peers = lax.axis_size(axis)
        if peers & (peers - 1):
            yield axis, 0
        else:
            by = 1
            while by < peers:
                yield axis, by
                by *= 2


def exchange(x, axis, by):
    if not by:
        return lax.psum(x.astype(F32), axis).astype(BF16) - x
    return lax.ppermute(x, axis, [(i, i ^ by) for i in range(lax.axis_size(axis))])


def shards(grad_out, activations, mixing, proj_tiles, proj_blocks, section_sizes):
    sections = lax.axis_size("pipe")
    section = lax.axis_index("pipe")
    micro, tokens, width = grad_out.shape
    slots = activations.shape[1]
    heads, head_size = mixing.shape[2:4]
    both = proj_tiles.shape[4]
    rank = both // 2
    scale = 1.0 / math.sqrt(tokens * lax.axis_size("dp"))
    pairs = sections // 2
    count = 4
    chunk = micro // count
    rows = chunk * tokens
    top_pair = pairs - 1
    last = None
    weights = iter(WORK)

    def call(kernel, name, ins, specs, outs, scratch=(), work=LIGHT, alias={}):
        outs = tuple(jax.ShapeDtypeStruct(s, t) for s, t in outs)
        return pl.pallas_call(
            kernel,
            out_shape=outs,
            in_specs=specs,
            out_specs=(VMEM,) * len(outs),
            scratch_shapes=scratch,
            input_output_aliases=alias,
            compiler_params=PARAMS,
            cost_estimate=pl.CostEstimate(flops=work, bytes_accessed=1000, transcendentals=0),
            name=name,
        )(*ins)

    def in_turn(kernel, name, first, ins, outs, more=(), scratch=(), work=LIGHT, alias=None):
        nonlocal last
        work = 10**6 * next(weights, 1)
        ins = [*first, last, *ins]
        res = call(kernel, name, ins, [VMEM] * len(ins), [*outs, (FLAG, F32), *more], scratch, work, alias or {})
        last = res[len(outs)]
        return [*res[: len(outs)], *res[len(outs) + 1 :]]

    step_outs = [((chunk, tokens, width), BF16), ((slots, rows, both), BF16)]
    slope_out = ((slots, chunk, tokens, width), F32)
    part_out = ((slots, rows, both), BF16)
    grad, proj, slope, part, next_slope, next_part, acts, top, mix_act, mix_grad, info = call(
        functools.partial(first_kernel, top_pair),
        "first",
        [
            pltpu.with_memory_space_constraint(x, pltpu.HBM)
            for x in (section_sizes, proj_blocks.transpose(1, 0, 2), grad_out, activations[0], mixing[0], proj_tiles[0])
        ],
        [HBM] * 6,
        [
            *step_outs,
            slope_out,
            part_out,
            slope_out,
            part_out,
            (activations.shape[1:], BF16),
            (grad_out.shape, BF16),
            ((slots, heads, head_size, head_size + both), BF16),
            ((slots, heads, head_size + both, head_size), BF16),
            (FLAG, F32),
        ],
        [
            pltpu.SMEM(section_sizes.shape, jnp.int32),
            pltpu.SMEM((slots, 1, proj_blocks.shape[2]), jnp.int32),
            pltpu.VMEM(proj_tiles.shape[1:], BF16),
            pltpu.SemaphoreType.DMA((6 * slots + 4,)),
        ],
    )
    last = info
    slopes = [slope, next_slope]
    swap = [(i, i ^ 1) for i in range(sections)]
    grads = [([], []) for _ in range(pairs)]
    projs = [([], []) for _ in range(pairs)]
    hops = [[] for _ in range(pairs)]
    core = [[] for _ in range(pairs)]

    def keep(p, odd, even, grad, proj):
        for parity, there in ((0, even), (1, odd)):
            if there:
                grads[p][parity].append(grad)
                projs[p][parity].append(proj)
        if odd:
            core[p].append(lax.ppermute(grad, "pipe", swap))
        if even and p + 1 < pairs:
            source = sections - 2 - 2 * p
            hop = [(source, source - 1)]
            if len(hops[p]) >= count - 2:
                hop = [(i, (i - 1) % sections) for i in range(sections)]
            hops[p].append(lax.ppermute(grad, "pipe", hop))

    def top_step(at):
        ins, scratch = [core[0][at - 1], slopes[at - 1]], []
        if at < count:
            ins += [top, acts, mix_act]
            scratch.append(pltpu.VMEM(slope_out[0], F32))
        kernel = functools.partial(top_kernel, top_pair, at, at < count)
        keep(0, at < count, True, *in_turn(kernel, "top", [info, mix_grad], ins, step_outs, scratch=scratch))

    def step(p, parity, at):
        source = hops[p - 1][at] if parity else core[p][at]
        kernel = functools.partial(step_kernel, top_pair - p, parity)
        keep(p, parity, not parity, *in_turn(kernel, "step", [info, mix_grad], [source, slopes[at]], step_outs))

    class Sum:
        def __init__(self, value, turns):
            self.mine, self.turns = value, turns
            self.go()

        def go(self):
            self.other = exchange(self.mine, *self.turns.pop(0))

        def turn(self, work=LIGHT):
            self.mine = in_turn(add_kernel, "add", [self.mine, self.other], [], [(self.mine.shape, BF16)], work=work)[0]
            self.go()

    def collect():
        ins = [grad for pair in grads for parity in (1, 0) for grad in pair[parity]]
        return in_turn(functools.partial(collect_kernel, pairs), "collect", [], ins, [(grad_out.shape, BF16)])[0]

    def sketch(group):
        out = ((slots, 2, rows, chunk * both), BF16)
        kernel = functools.partial(widen_kernel, group, chunk)
        wide = in_turn(kernel, "widen", [act_sum.mine, act_sum.other], [], [out])[0]
        ins = []
        for p in range(pairs):
            for parity in (1, 0):
                ins += projs[p][parity][2 * group : 2 * group + 2]
        kernel = functools.partial(sketch_kernel, pairs, scale)
        out = ((slots, 2 * chunk, rank // 2, both), BF16)
        return in_turn(kernel, "sketch", [info], [*ins, wide], [out])[0]

    low = pairs - 1
    act_turns = list(swaps(("tensor",)))
    turns = list(swaps(("dp", "tensor")))
    keep(0, True, False, grad, proj)
    slope, act_part = in_turn(
        functools.partial(beside_kernel, top_pair),
        "beside",
        [info, acts, mix_act],
        [part, next_part],
        [slope_out, ((2, *part_out[0]), BF16)],
        scratch=[pltpu.VMEM(*part_out)],
    )
    slopes.append(slope)
    act_sum = Sum(act_part, act_turns)
    top_step(1)
    top_step(2)
    kernel = functools.partial(slope_kernel, top_pair, 3 * chunk)
    slopes += in_turn(kernel, "slope", [info, acts, mix_act], [], [slope_out])
    while act_sum.turns:
        act_sum.turn()
    top_step(3)
    for p in range(1, pairs):
        step(p, 1, 0)
        if p == 1:
            top_step(count)
        else:
            step(p - 1, 0, 3)
        step(p, 1, 1)
        step(p, 0, 0)
        step(p, 0, 1)
        if p < low:
            step(p, 1, 2)
            step(p, 1, 3)
            step(p, 0, 2)
    early = Sum(sketch(0), list(swaps(("tensor", "dp"))))
    step(low, 1, 2)
    step(low, 1, 3)
    step(low, 0, 2)
    step(low, 0, 3)
    late = Sum(sketch(1), list(turns))
    segment_out = None
    while late.turns:
        if early.turns:
            early.turn()
        late.turn()
        if segment_out is None:
            segment_out = collect()
    ins = [last, early.mine, early.other, late.mine, late.other]
    (total,) = call(last_kernel, "last", ins, [VMEM] * 5, [((slots, micro, rank * rank), F32)])

    return (segment_out[None], total[None])


def solution(mesh):
    return jax.shard_map(
        shards,
        mesh=mesh,
        in_specs=(
            P(None, "dp", "tensor"),
            P("pipe", None, None, "dp", "tensor"),
            P("pipe", None, "tensor", None, None),
            P("pipe", None, None, None, None),
            P("pipe", None, None),
            P(),
        ),
        out_specs=(P("pipe", None, "dp", "tensor"), P("pipe", None, None, None)),
        check_vma=False,
    )
```

profile of v0, /device:TPU:0, one launch (start us, length us, event | category | flops | bytes accessed | tf_op | source)
XLA Modules:
  0.0 50.9 jit_solution(8062125731631983142)
XLA Ops:
  0.6 3.2 %first.1 = (bf16[2,64,1024]{2,1,0:T(8,128)(2,1)S(1)}, bf16[3,128,128]{2,1,0:T(8,128)(2,1)S(1)}, f32[3,2,64,1024]{3,2,1,0:T(8,128)S(1)}, bf16[3,128,128]{2,1,0:T(...) custom-call(s32[4]{0:T(128)} %sizes_in.1, ...), custom_call_target="tpu_custom_call" | custom-call | flops 1000 | bytes 1000 | tf_op jit(solution)/shard_map/first/pallas_call | solution.py:371
  3.9 0.5 %collective-permute-start.1 = (bf16[2,64,1024]{2,1,0:T(8,128)(2,1)S(1)}, bf16[2,64,1024]{2,1,0:T(8,128)(2,1)S(1)}, u32[]{:S(2)}, u32[]{:S(2)}) collective-permute-start(bf16[2,64,1024]{2,1,0:T(8,128)(2,1)S(1)} %get-tuple-element.82.refs_0_), channel_id=1, source_target_pairs={{0,4},{4,0},{8,12},{12,8},{1,5},{5,1},{9,13},{13,9},{2,6},{6,2},{1... | collective-permute-start | bytes 786440 | tf_op jit(solution)/shard_map/ppermute | solution.py:435
  4.4 0.5 %beside.1 = (f32[3,2,64,1024]{3,2,1,0:T(8,128)S(1)}, bf16[2,3,128,128]{3,2,1,0:T(8,128)(2,1)S(1)}, f32[8,128]{1,0:T(8,128)S(1)}) custom-call(f32[8,128]{1,0:T(8,128)S(1)} %get-tuple-element.74.info.after, bf16[3,8,64,1024]{3,2,1,0:T(8,128)(2,1)S(1)} %get-tuple-element.75.acts.refs_1_, bf16[3,8,128,256]{3,2,1,0:T(8,128)(2,1)S(1)} %get-tuple-element.76.mix_act.refs_2_, ...), custom_call_target="tpu_custom_call" | custom-call | flops 3000000000 | bytes 1000 | tf_op jit(solution)/shard_map/beside/pallas_call | solution.py:371
  4.9 0.6 %collective-permute-done.1.even_in = bf16[2,64,1024]{2,1,0:T(8,128)(2,1)S(1)} collective-permute-done((bf16[2,64,1024]{2,1,0:T(8,128)(2,1)S(1)}, bf16[2,64,1024]{2,1,0:T(8,128)(2,1)S(1)}, u32[]{:S(2)}, u32[]{:S(2)}) %collective-permute-start.1) | collective-permute-done | bytes 262176 | tf_op jit(solution)/shard_map/ppermute | solution.py:435
  5.5 0.4 collective-permute-start.2
  5.9 2.7 %collective-permute-start = (bf16[2,3,128,128]{3,2,1,0:T(8,128)(2,1)S(1)}, bf16[2,3,128,128]{3,2,1,0:T(8,128)(2,1)S(1)}, u32[]{:S(2)}, u32[]{:S(2)}) collective-permute-start(bf16[2,3,128,128]{3,2,1,0:T(8,128)(2,1)S(1)} %get-tuple-element.79.mine), channel_id=1, source_target_pairs={{0,1},{1,0},{2,3},{3,2},{4,5},{5,4},{6,7},{7,6},{8,9},{9,8},{10,11... | collective-permute-start | bytes 589832 | tf_op jit(solution)/shard_map/ppermute | solution.py:349
  8.6 0.7 %collective-permute-start.5 = (bf16[2,64,1024]{2,1,0:T(8,128)(2,1)S(1)}, bf16[2,64,1024]{2,1,0:T(8,128)(2,1)S(1)}, u32[]{:S(2)}, u32[]{:S(2)}) collective-permute-start(bf16[2,64,1024]{2,1,0:T(8,128)(2,1)S(1)} %get-tuple-element.86.refs_1_.refs_4_), channel_id=1, source_target_pairs={{8,4},{9,5},{10,6},{11,7},{24,20},{25,21},{26,22},{27,23}} | collective-permute-start | bytes 786440 | tf_op jit(solution)/shard_map/ppermute | solution.py:441
  9.3 0.0 collective-permute-done.2.even_in
  9.4 0.8 %collective-permute-start.4 = (bf16[2,64,1024]{2,1,0:T(8,128)(2,1)S(1)}, bf16[2,64,1024]{2,1,0:T(8,128)(2,1)S(1)}, u32[]{:S(2)}, u32[]{:S(2)}) collective-permute-start(bf16[2,64,1024]{2,1,0:T(8,128)(2,1)S(1)} %get-tuple-element.92.refs_2_.refs_5_), channel_id=1, source_target_pairs={{0,4},{4,0},{8,12},{12,8},{1,5},{5,1},{9,13},{13,9},{2,6},{6,2},{1... | collective-permute-start | bytes 786440 | tf_op jit(solution)/shard_map/ppermute | solution.py:435
  10.1 0.7 %collective-permute-start.7 = (bf16[2,64,1024]{2,1,0:T(8,128)(2,1)S(1)}, bf16[2,64,1024]{2,1,0:T(8,128)(2,1)S(1)}, u32[]{:S(2)}, u32[]{:S(2)}) collective-permute-start(bf16[2,64,1024]{2,1,0:T(8,128)(2,1)S(1)} %get-tuple-element.92.refs_2_.refs_5_), channel_id=1, source_target_pairs={{8,4},{9,5},{10,6},{11,7},{24,20},{25,21},{26,22},{27,23}} | collective-permute-start | bytes 786440 | tf_op jit(solution)/shard_map/ppermute | solution.py:441
  10.8 0.4 slope.1
  11.2 2.8 %collective-permute-done.other = bf16[2,3,128,128]{3,2,1,0:T(8,128)(2,1)S(1)} collective-permute-done((bf16[2,3,128,128]{3,2,1,0:T(8,128)(2,1)S(1)}, bf16[2,3,128,128]{3,2,1,0:T(8,128)(2,1)S(1)}, u32[]{:S(2)}, u32[]{:S(2)}) %collective-permute-start) | collective-permute-done | bytes 196640 | tf_op jit(solution)/shard_map/ppermute | solution.py:349
  14.1 2.8 %collective-permute-start.3 = (bf16[2,3,128,128]{3,2,1,0:T(8,128)(2,1)S(1)}, bf16[2,3,128,128]{3,2,1,0:T(8,128)(2,1)S(1)}, u32[]{:S(2)}, u32[]{:S(2)}) collective-permute-start(bf16[2,3,128,128]{3,2,1,0:T(8,128)(2,1)S(1)} %get-tuple-element.90.mine), channel_id=1, source_target_pairs={{0,2},{1,3},{2,0},{3,1},{4,6},{5,7},{6,4},{7,5},{8,10},{9,11},{10,... | collective-permute-start | bytes 589832 | tf_op jit(solution)/shard_map/ppermute | solution.py:349
  16.9 0.0 collective-permute-done.4.even_in
  16.9 0.0 collective-permute-start.6
  16.9 6.1 %collective-permute-start.10 = (bf16[2,64,1024]{2,1,0:T(8,128)(2,1)S(1)}, bf16[2,64,1024]{2,1,0:T(8,128)(2,1)S(1)}, u32[]{:S(2)}, u32[]{:S(2)}) collective-permute-start(bf16[2,64,1024]{2,1,0:T(8,128)(2,1)S(1)} %get-tuple-element.96.refs_3_.refs_6_), channel_id=1, source_target_pairs={{0,12},{4,0},{8,4},{12,8},{1,13},{5,1},{9,5},{13,9},{2,14},{6,2},{... | collective-permute-start | bytes 786440 | tf_op jit(solution)/shard_map/ppermute | solution.py:441
  23.0 0.0 collective-permute-done.5.source
  23.1 0.0 collective-permute-start.8
  23.1 0.0 collective-permute-done.6.even_in
  23.1 0.0 collective-permute-done.7.source
  23.1 0.2 step.9
  23.3 0.9 %collective-permute-start.9 = (bf16[2,64,1024]{2,1,0:T(8,128)(2,1)S(1)}, bf16[2,64,1024]{2,1,0:T(8,128)(2,1)S(1)}, u32[]{:S(2)}, u32[]{:S(2)}) collective-permute-start(bf16[2,64,1024]{2,1,0:T(8,128)(2,1)S(1)} %get-tuple-element.102.refs_9_), channel_id=1, source_target_pairs={{0,4},{4,0},{8,12},{12,8},{1,5},{5,1},{9,13},{13,9},{2,6},{6,2},{1... | collective-permute-start | bytes 786440 | tf_op jit(solution)/shard_map/ppermute | solution.py:435
  24.2 1.7 %collective-permute-start.11 = (bf16[2,64,1024]{2,1,0:T(8,128)(2,1)S(1)}, bf16[2,64,1024]{2,1,0:T(8,128)(2,1)S(1)}, u32[]{:S(2)}, u32[]{:S(2)}) collective-permute-start(bf16[2,64,1024]{2,1,0:T(8,128)(2,1)S(1)} %get-tuple-element.115.refs_7_), channel_id=1, source_target_pairs={{0,12},{4,0},{8,4},{12,8},{1,13},{5,1},{9,5},{13,9},{2,14},{6,2},{... | collective-permute-start | bytes 786440 | tf_op jit(solution)/shard_map/ppermute | solution.py:441
  25.9 0.4 step.10
  26.4 0.4 step.11
  26.8 0.0 collective-permute-done.3.other
  26.8 0.1 widen.2
  26.9 0.5 %sketch.2 = (bf16[3,4,32,128]{3,2,1,0:T(8,128)(2,1)S(1)}, f32[8,128]{1,0:T(8,128)S(1)}) custom-call(f32[8,128]{1,0:T(8,128)S(1)} %get-tuple-element.74.info.after, f32[8,128]{1,0:T(8,128)S(1)} %get-tuple-element.104.after, bf16[3,128,128]{2,1,0:T(8,128)(2,1)S(1)} %get-tuple-element.105.refs_0_, bf16[3,128,128]{2,1,0:T(8,128)(2,1)S(1)} %get-tuple-element.106.refs_1_.refs_2_, ...), custom_call_target="tpu_custom_call" | custom-call | flops 2000000000 | bytes 1000 | tf_op jit(solution)/shard_map/sketch/pallas_call | solution.py:371
  27.5 0.1 collective-permute-start.12
  27.7 2.1 %collective-permute-done.11.source = bf16[2,64,1024]{2,1,0:T(8,128)(2,1)S(1)} collective-permute-done((bf16[2,64,1024]{2,1,0:T(8,128)(2,1)S(1)}, bf16[2,64,1024]{2,1,0:T(8,128)(2,1)S(1)}, u32[]{:S(2)}, u32[]{:S(2)}) %collective-permute-start.11) | collective-permute-done | bytes 262176 | tf_op jit(solution)/shard_map/ppermute | solution.py:441
  29.8 0.8 %collective-permute-start.13 = (bf16[2,64,1024]{2,1,0:T(8,128)(2,1)S(1)}, bf16[2,64,1024]{2,1,0:T(8,128)(2,1)S(1)}, u32[]{:S(2)}, u32[]{:S(2)}) collective-permute-start(bf16[2,64,1024]{2,1,0:T(8,128)(2,1)S(1)} %get-tuple-element.119.refs_11_), channel_id=1, source_target_pairs={{0,4},{4,0},{8,12},{12,8},{1,5},{5,1},{9,13},{13,9},{2,6},{6,2},{1... | collective-permute-start | bytes 786440 | tf_op jit(solution)/shard_map/ppermute | solution.py:435
  30.6 1.7 %collective-permute-start.15 = (bf16[3,4,32,128]{3,2,1,0:T(8,128)(2,1)S(1)}, bf16[3,4,32,128]{3,2,1,0:T(8,128)(2,1)S(1)}, u32[]{:S(2)}, u32[]{:S(2)}) collective-permute-start(bf16[3,4,32,128]{3,2,1,0:T(8,128)(2,1)S(1)} %get-tuple-element.130.mine), channel_id=1, source_target_pairs={{0,1},{1,0},{2,3},{3,2},{4,5},{5,4},{6,7},{7,6},{8,9},{9,8},{10,11... | collective-permute-start | bytes 294920 | tf_op jit(solution)/shard_map/ppermute | solution.py:349
  32.3 0.0 collective-permute-done.12.source
  32.4 0.4 step.14
  32.8 0.4 step.15
  33.3 0.1 widen.3
  33.4 0.5 %sketch.3 = (bf16[3,4,32,128]{3,2,1,0:T(8,128)(2,1)S(1)}, f32[8,128]{1,0:T(8,128)S(1)}) custom-call(f32[8,128]{1,0:T(8,128)S(1)} %get-tuple-element.74.info.after, f32[8,128]{1,0:T(8,128)S(1)} %get-tuple-element.121.after, bf16[3,128,128]{2,1,0:T(8,128)(2,1)S(1)} %get-tuple-element.107.refs_3_.refs_0_, ...), custom_call_target="tpu_custom_call" | custom-call | flops 1000000 | bytes 1000 | tf_op jit(solution)/shard_map/sketch/pallas_call | solution.py:371
  33.9 1.6 %collective-permute-start.14 = (bf16[3,4,32,128]{3,2,1,0:T(8,128)(2,1)S(1)}, bf16[3,4,32,128]{3,2,1,0:T(8,128)(2,1)S(1)}, u32[]{:S(2)}, u32[]{:S(2)}) collective-permute-start(bf16[3,4,32,128]{3,2,1,0:T(8,128)(2,1)S(1)} %get-tuple-element.129.mine), channel_id=1, source_target_pairs={{0,16},{16,0},{1,17},{17,1},{2,18},{18,2},{3,19},{19,3},{4,20},{20... | collective-permute-start | bytes 294920 | tf_op jit(solution)/shard_map/ppermute | solution.py:349
  35.5 1.2 %collective-permute-start.17 = (bf16[3,4,32,128]{3,2,1,0:T(8,128)(2,1)S(1)}, bf16[3,4,32,128]{3,2,1,0:T(8,128)(2,1)S(1)}, u32[]{:S(2)}, u32[]{:S(2)}) collective-permute-start(bf16[3,4,32,128]{3,2,1,0:T(8,128)(2,1)S(1)} %get-tuple-element.140.mine), channel_id=1, source_target_pairs={{0,2},{1,3},{2,0},{3,1},{4,6},{5,7},{6,4},{7,5},{8,10},{9,11},{10,... | collective-permute-start | bytes 294920 | tf_op jit(solution)/shard_map/ppermute | solution.py:349
  36.7 1.9 %collective-permute-done.14.other = bf16[3,4,32,128]{3,2,1,0:T(8,128)(2,1)S(1)} collective-permute-done((bf16[3,4,32,128]{3,2,1,0:T(8,128)(2,1)S(1)}, bf16[3,4,32,128]{3,2,1,0:T(8,128)(2,1)S(1)}, u32[]{:S(2)}, u32[]{:S(2)}) %collective-permute-start.14) | collective-permute-done | bytes 98336 | tf_op jit(solution)/shard_map/ppermute | solution.py:349
  38.6 0.8 %collective-permute-start.16 = (bf16[3,4,32,128]{3,2,1,0:T(8,128)(2,1)S(1)}, bf16[3,4,32,128]{3,2,1,0:T(8,128)(2,1)S(1)}, u32[]{:S(2)}, u32[]{:S(2)}) collective-permute-start(bf16[3,4,32,128]{3,2,1,0:T(8,128)(2,1)S(1)} %get-tuple-element.139.mine), channel_id=1, source_target_pairs={{0,1},{1,0},{2,3},{3,2},{4,5},{5,4},{6,7},{7,6},{8,9},{9,8},{10,11... | collective-permute-start | bytes 294920 | tf_op jit(solution)/shard_map/ppermute | solution.py:349
  39.4 1.0 %collect.1 = (bf16[8,64,1024]{2,1,0:T(8,128)(2,1)}, f32[8,128]{1,0:T(8,128)S(1)}) custom-call(f32[8,128]{1,0:T(8,128)S(1)} %get-tuple-element.133.after, bf16[2,64,1024]{2,1,0:T(8,128)(2,1)S(1)} %get-tuple-element.82.refs_0_, bf16[2,64,1024]{2,1,0:T(8,128)(2,1)S(1)} %get-tuple-element.86.refs_1_.refs_4_, ...), custom_call_target="tpu_custom_call" | custom-call | flops 10000000000 | bytes 1000 | tf_op jit(solution)/shard_map/collect/pallas_call | solution.py:371
  40.5 1.4 %collective-permute-done.17.other = bf16[3,4,32,128]{3,2,1,0:T(8,128)(2,1)S(1)} collective-permute-done((bf16[3,4,32,128]{3,2,1,0:T(8,128)(2,1)S(1)}, bf16[3,4,32,128]{3,2,1,0:T(8,128)(2,1)S(1)}, u32[]{:S(2)}, u32[]{:S(2)}) %collective-permute-start.17) | collective-permute-done | bytes 98336 | tf_op jit(solution)/shard_map/ppermute | solution.py:349
  41.8 1.6 %collective-permute-start.18 = (bf16[3,4,32,128]{3,2,1,0:T(8,128)(2,1)S(1)}, bf16[3,4,32,128]{3,2,1,0:T(8,128)(2,1)S(1)}, u32[]{:S(2)}, u32[]{:S(2)}) collective-permute-start(bf16[3,4,32,128]{3,2,1,0:T(8,128)(2,1)S(1)} %get-tuple-element.144.refs_0_), channel_id=1, source_target_pairs={{0,16},{16,0},{1,17},{17,1},{2,18},{18,2},{3,19},{19,3},{4,20},{20... | collective-permute-start | bytes 294920 | tf_op jit(solution)/shard_map/ppermute | solution.py:349
  43.4 0.8 %collective-permute-start.19 = (bf16[3,4,32,128]{3,2,1,0:T(8,128)(2,1)S(1)}, bf16[3,4,32,128]{3,2,1,0:T(8,128)(2,1)S(1)}, u32[]{:S(2)}, u32[]{:S(2)}) collective-permute-start(bf16[3,4,32,128]{3,2,1,0:T(8,128)(2,1)S(1)} %get-tuple-element.145.refs_2_), channel_id=1, source_target_pairs={{0,2},{1,3},{2,0},{3,1},{4,6},{5,7},{6,4},{7,5},{8,10},{9,11},{10,... | collective-permute-start | bytes 294920 | tf_op jit(solution)/shard_map/ppermute | solution.py:349
  44.3 2.3 %collective-permute-done.18.refs_1_ = bf16[3,4,32,128]{3,2,1,0:T(8,128)(2,1)S(1)} collective-permute-done((bf16[3,4,32,128]{3,2,1,0:T(8,128)(2,1)S(1)}, bf16[3,4,32,128]{3,2,1,0:T(8,128)(2,1)S(1)}, u32[]{:S(2)}, u32[]{:S(2)}) %collective-permute-start.18) | collective-permute-done | bytes 98336 | tf_op jit(solution)/shard_map/ppermute | solution.py:349
  46.5 3.5 %collective-permute-done.19.refs_3_ = bf16[3,4,32,128]{3,2,1,0:T(8,128)(2,1)S(1)} collective-permute-done((bf16[3,4,32,128]{3,2,1,0:T(8,128)(2,1)S(1)}, bf16[3,4,32,128]{3,2,1,0:T(8,128)(2,1)S(1)}, u32[]{:S(2)}, u32[]{:S(2)}) %collective-permute-start.19) | collective-permute-done | bytes 98336 | tf_op jit(solution)/shard_map/ppermute | solution.py:349
  50.1 0.9 %last.1 = f32[3,8,4096]{2,1,0:T(8,128)} custom-call(f32[8,128]{1,0:T(8,128)S(1)} %get-tuple-element.143.after, bf16[3,4,32,128]{3,2,1,0:T(8,128)(2,1)S(1)} %get-tuple-element.144.refs_0_, bf16[3,4,32,128]{3,2,1,0:T(8,128)(2,1)S(1)} %collective-permute-done.18.refs_1_, bf16[3,4,32,128]{3,2,1,0:T(8,128)(2,1)S(1)} %get-tuple-element.145.refs_2_, ...), custom_call_target="tpu_custom_call" | custom-call | flops 1000 | bytes 1000 | tf_op jit(solution)/shard_map/last/pallas_call | solution.py:371
  (18 shorter events, 0.3 us)
Async XLA Ops:
  3.9 1.7 %collective-permute-start.1 = (bf16[2,64,1024]{2,1,0:T(8,128)(2,1)S(1)}, bf16[2,64,1024]{2,1,0:T(8,128)(2,1)S(1)}, u32[]{:S(2)}, u32[]{:S(2)}) collective-permute-start(bf16[2,64,1024]{2,1,0:T(8,128)(2,1)S(1)} %get-tuple-element.82.refs_0_), channel_id=1, source_target_pairs={{0,4},{4,0},{8,12},{12,8},{1,5},{5,1},{9,13},{13,9},{2,6},{6,2},{1... | collective-permute-start | bytes 786440 | tf_op jit(solution)/shard_map/ppermute | solution.py:435
  5.5 3.8 %collective-permute-start.2 = (bf16[2,64,1024]{2,1,0:T(8,128)(2,1)S(1)}, bf16[2,64,1024]{2,1,0:T(8,128)(2,1)S(1)}, u32[]{:S(2)}, u32[]{:S(2)}) collective-permute-start(bf16[2,64,1024]{2,1,0:T(8,128)(2,1)S(1)} %get-tuple-element.86.refs_1_.refs_4_), channel_id=1, source_target_pairs={{0,4},{4,0},{8,12},{12,8},{1,5},{5,1},{9,13},{13,9},{2,6},{6,2},{1... | collective-permute-start | bytes 786440 | tf_op jit(solution)/shard_map/ppermute | solution.py:435
  5.9 8.1 %collective-permute-start = (bf16[2,3,128,128]{3,2,1,0:T(8,128)(2,1)S(1)}, bf16[2,3,128,128]{3,2,1,0:T(8,128)(2,1)S(1)}, u32[]{:S(2)}, u32[]{:S(2)}) collective-permute-start(bf16[2,3,128,128]{3,2,1,0:T(8,128)(2,1)S(1)} %get-tuple-element.79.mine), channel_id=1, source_target_pairs={{0,1},{1,0},{2,3},{3,2},{4,5},{5,4},{6,7},{7,6},{8,9},{9,8},{10,11... | collective-permute-start | bytes 589832 | tf_op jit(solution)/shard_map/ppermute | solution.py:349
  8.6 14.4 %collective-permute-start.5 = (bf16[2,64,1024]{2,1,0:T(8,128)(2,1)S(1)}, bf16[2,64,1024]{2,1,0:T(8,128)(2,1)S(1)}, u32[]{:S(2)}, u32[]{:S(2)}) collective-permute-start(bf16[2,64,1024]{2,1,0:T(8,128)(2,1)S(1)} %get-tuple-element.86.refs_1_.refs_4_), channel_id=1, source_target_pairs={{8,4},{9,5},{10,6},{11,7},{24,20},{25,21},{26,22},{27,23}} | collective-permute-start | bytes 786440 | tf_op jit(solution)/shard_map/ppermute | solution.py:441
  9.4 7.6 %collective-permute-start.4 = (bf16[2,64,1024]{2,1,0:T(8,128)(2,1)S(1)}, bf16[2,64,1024]{2,1,0:T(8,128)(2,1)S(1)}, u32[]{:S(2)}, u32[]{:S(2)}) collective-permute-start(bf16[2,64,1024]{2,1,0:T(8,128)(2,1)S(1)} %get-tuple-element.92.refs_2_.refs_5_), channel_id=1, source_target_pairs={{0,4},{4,0},{8,12},{12,8},{1,5},{5,1},{9,13},{13,9},{2,6},{6,2},{1... | collective-permute-start | bytes 786440 | tf_op jit(solution)/shard_map/ppermute | solution.py:435
  10.1 13.0 %collective-permute-start.7 = (bf16[2,64,1024]{2,1,0:T(8,128)(2,1)S(1)}, bf16[2,64,1024]{2,1,0:T(8,128)(2,1)S(1)}, u32[]{:S(2)}, u32[]{:S(2)}) collective-permute-start(bf16[2,64,1024]{2,1,0:T(8,128)(2,1)S(1)} %get-tuple-element.92.refs_2_.refs_5_), channel_id=1, source_target_pairs={{8,4},{9,5},{10,6},{11,7},{24,20},{25,21},{26,22},{27,23}} | collective-permute-start | bytes 786440 | tf_op jit(solution)/shard_map/ppermute | solution.py:441
  14.1 12.7 %collective-permute-start.3 = (bf16[2,3,128,128]{3,2,1,0:T(8,128)(2,1)S(1)}, bf16[2,3,128,128]{3,2,1,0:T(8,128)(2,1)S(1)}, u32[]{:S(2)}, u32[]{:S(2)}) collective-permute-start(bf16[2,3,128,128]{3,2,1,0:T(8,128)(2,1)S(1)} %get-tuple-element.90.mine), channel_id=1, source_target_pairs={{0,2},{1,3},{2,0},{3,1},{4,6},{5,7},{6,4},{7,5},{8,10},{9,11},{10,... | collective-permute-start | bytes 589832 | tf_op jit(solution)/shard_map/ppermute | solution.py:349
  16.9 6.1 %collective-permute-start.6 = (bf16[2,64,1024]{2,1,0:T(8,128)(2,1)S(1)}, bf16[2,64,1024]{2,1,0:T(8,128)(2,1)S(1)}, u32[]{:S(2)}, u32[]{:S(2)}) collective-permute-start(bf16[2,64,1024]{2,1,0:T(8,128)(2,1)S(1)} %get-tuple-element.96.refs_3_.refs_6_), channel_id=1, source_target_pairs={{0,4},{4,0},{8,12},{12,8},{1,5},{5,1},{9,13},{13,9},{2,6},{6,2},{1... | collective-permute-start | bytes 786440 | tf_op jit(solution)/shard_map/ppermute | solution.py:435
  16.9 10.6 %collective-permute-start.10 = (bf16[2,64,1024]{2,1,0:T(8,128)(2,1)S(1)}, bf16[2,64,1024]{2,1,0:T(8,128)(2,1)S(1)}, u32[]{:S(2)}, u32[]{:S(2)}) collective-permute-start(bf16[2,64,1024]{2,1,0:T(8,128)(2,1)S(1)} %get-tuple-element.96.refs_3_.refs_6_), channel_id=1, source_target_pairs={{0,12},{4,0},{8,4},{12,8},{1,13},{5,1},{9,5},{13,9},{2,14},{6,2},{... | collective-permute-start | bytes 786440 | tf_op jit(solution)/shard_map/ppermute | solution.py:441
  23.1 2.9 %collective-permute-start.8 = (bf16[2,64,1024]{2,1,0:T(8,128)(2,1)S(1)}, bf16[2,64,1024]{2,1,0:T(8,128)(2,1)S(1)}, u32[]{:S(2)}, u32[]{:S(2)}) collective-permute-start(bf16[2,64,1024]{2,1,0:T(8,128)(2,1)S(1)} %get-tuple-element.100.refs_8_), channel_id=1, source_target_pairs={{0,4},{4,0},{8,12},{12,8},{1,5},{5,1},{9,13},{13,9},{2,6},{6,2},{1... | collective-permute-start | bytes 786440 | tf_op jit(solution)/shard_map/ppermute | solution.py:435
  23.3 3.0 %collective-permute-start.9 = (bf16[2,64,1024]{2,1,0:T(8,128)(2,1)S(1)}, bf16[2,64,1024]{2,1,0:T(8,128)(2,1)S(1)}, u32[]{:S(2)}, u32[]{:S(2)}) collective-permute-start(bf16[2,64,1024]{2,1,0:T(8,128)(2,1)S(1)} %get-tuple-element.102.refs_9_), channel_id=1, source_target_pairs={{0,4},{4,0},{8,12},{12,8},{1,5},{5,1},{9,13},{13,9},{2,6},{6,2},{1... | collective-permute-start | bytes 786440 | tf_op jit(solution)/shard_map/ppermute | solution.py:435
  24.2 5.6 %collective-permute-start.11 = (bf16[2,64,1024]{2,1,0:T(8,128)(2,1)S(1)}, bf16[2,64,1024]{2,1,0:T(8,128)(2,1)S(1)}, u32[]{:S(2)}, u32[]{:S(2)}) collective-permute-start(bf16[2,64,1024]{2,1,0:T(8,128)(2,1)S(1)} %get-tuple-element.115.refs_7_), channel_id=1, source_target_pairs={{0,12},{4,0},{8,4},{12,8},{1,13},{5,1},{9,5},{13,9},{2,14},{6,2},{... | collective-permute-start | bytes 786440 | tf_op jit(solution)/shard_map/ppermute | solution.py:441
  27.5 4.8 %collective-permute-start.12 = (bf16[2,64,1024]{2,1,0:T(8,128)(2,1)S(1)}, bf16[2,64,1024]{2,1,0:T(8,128)(2,1)S(1)}, u32[]{:S(2)}, u32[]{:S(2)}) collective-permute-start(bf16[2,64,1024]{2,1,0:T(8,128)(2,1)S(1)} %get-tuple-element.117.refs_10_), channel_id=1, source_target_pairs={{0,4},{4,0},{8,12},{12,8},{1,5},{5,1},{9,13},{13,9},{2,6},{6,2},{1... | collective-permute-start | bytes 786440 | tf_op jit(solution)/shard_map/ppermute | solution.py:435
  29.8 3.0 %collective-permute-start.13 = (bf16[2,64,1024]{2,1,0:T(8,128)(2,1)S(1)}, bf16[2,64,1024]{2,1,0:T(8,128)(2,1)S(1)}, u32[]{:S(2)}, u32[]{:S(2)}) collective-permute-start(bf16[2,64,1024]{2,1,0:T(8,128)(2,1)S(1)} %get-tuple-element.119.refs_11_), channel_id=1, source_target_pairs={{0,4},{4,0},{8,12},{12,8},{1,5},{5,1},{9,13},{13,9},{2,6},{6,2},{1... | collective-permute-start | bytes 786440 | tf_op jit(solution)/shard_map/ppermute | solution.py:435
  30.6 4.9 %collective-permute-start.15 = (bf16[3,4,32,128]{3,2,1,0:T(8,128)(2,1)S(1)}, bf16[3,4,32,128]{3,2,1,0:T(8,128)(2,1)S(1)}, u32[]{:S(2)}, u32[]{:S(2)}) collective-permute-start(bf16[3,4,32,128]{3,2,1,0:T(8,128)(2,1)S(1)} %get-tuple-element.130.mine), channel_id=1, source_target_pairs={{0,1},{1,0},{2,3},{3,2},{4,5},{5,4},{6,7},{7,6},{8,9},{9,8},{10,11... | collective-permute-start | bytes 294920 | tf_op jit(solution)/shard_map/ppermute | solution.py:349
  33.9 4.7 %collective-permute-start.14 = (bf16[3,4,32,128]{3,2,1,0:T(8,128)(2,1)S(1)}, bf16[3,4,32,128]{3,2,1,0:T(8,128)(2,1)S(1)}, u32[]{:S(2)}, u32[]{:S(2)}) collective-permute-start(bf16[3,4,32,128]{3,2,1,0:T(8,128)(2,1)S(1)} %get-tuple-element.129.mine), channel_id=1, source_target_pairs={{0,16},{16,0},{1,17},{17,1},{2,18},{18,2},{3,19},{19,3},{4,20},{20... | collective-permute-start | bytes 294920 | tf_op jit(solution)/shard_map/ppermute | solution.py:349
  35.5 6.3 %collective-permute-start.17 = (bf16[3,4,32,128]{3,2,1,0:T(8,128)(2,1)S(1)}, bf16[3,4,32,128]{3,2,1,0:T(8,128)(2,1)S(1)}, u32[]{:S(2)}, u32[]{:S(2)}) collective-permute-start(bf16[3,4,32,128]{3,2,1,0:T(8,128)(2,1)S(1)} %get-tuple-element.140.mine), channel_id=1, source_target_pairs={{0,2},{1,3},{2,0},{3,1},{4,6},{5,7},{6,4},{7,5},{8,10},{9,11},{10,... | collective-permute-start | bytes 294920 | tf_op jit(solution)/shard_map/ppermute | solution.py:349
  38.6 4.8 %collective-permute-start.16 = (bf16[3,4,32,128]{3,2,1,0:T(8,128)(2,1)S(1)}, bf16[3,4,32,128]{3,2,1,0:T(8,128)(2,1)S(1)}, u32[]{:S(2)}, u32[]{:S(2)}) collective-permute-start(bf16[3,4,32,128]{3,2,1,0:T(8,128)(2,1)S(1)} %get-tuple-element.139.mine), channel_id=1, source_target_pairs={{0,1},{1,0},{2,3},{3,2},{4,5},{5,4},{6,7},{7,6},{8,9},{9,8},{10,11... | collective-permute-start | bytes 294920 | tf_op jit(solution)/shard_map/ppermute | solution.py:349
  41.8 4.7 %collective-permute-start.18 = (bf16[3,4,32,128]{3,2,1,0:T(8,128)(2,1)S(1)}, bf16[3,4,32,128]{3,2,1,0:T(8,128)(2,1)S(1)}, u32[]{:S(2)}, u32[]{:S(2)}) collective-permute-start(bf16[3,4,32,128]{3,2,1,0:T(8,128)(2,1)S(1)} %get-tuple-element.144.refs_0_), channel_id=1, source_target_pairs={{0,16},{16,0},{1,17},{17,1},{2,18},{18,2},{3,19},{19,3},{4,20},{20... | collective-permute-start | bytes 294920 | tf_op jit(solution)/shard_map/ppermute | solution.py:349
  43.4 6.6 %collective-permute-start.19 = (bf16[3,4,32,128]{3,2,1,0:T(8,128)(2,1)S(1)}, bf16[3,4,32,128]{3,2,1,0:T(8,128)(2,1)S(1)}, u32[]{:S(2)}, u32[]{:S(2)}) collective-permute-start(bf16[3,4,32,128]{3,2,1,0:T(8,128)(2,1)S(1)} %get-tuple-element.145.refs_2_), channel_id=1, source_target_pairs={{0,2},{1,3},{2,0},{3,1},{4,6},{5,7},{6,4},{7,5},{8,10},{9,11},{10,... | collective-permute-start | bytes 294920 | tf_op jit(solution)/shard_map/ppermute | solution.py:349
where the time goes:
time: 51.2 us; the launch traced here: 50.9 us
  starting transfers between devices  25.8 us (50%)
  waiting for transfers between devices  14.7 us (29%)
  Pallas kernels  9.57 us (19%)
  between operations  0.84 us (2%)
    ppermute x8, starting transfers between devices, exchange(): lax.ppermute(x, axis, [(i, i ^ by) for i in range(lax.axis_size(axis))])  13.2 us
    ppermute x8, waiting for transfers between devices, exchange(): lax.ppermute(x, axis, [(i, i ^ by) for i in range(lax.axis_size(axis))])  11.9 us
    pallas_call x26, Pallas kernels, call(): pl.pallas_call(kernel, out_shape=outs, in_specs=specs, out_specs=(VMEM,)...  9.57 us
    ppermute x4, starting transfers between devices, keep(): hops[p].append(lax.ppermute(grad, 'pipe', hop))  9.11 us
    ppermute x8, starting transfers between devices, keep(): core[p].append(lax.ppermute(grad, 'pipe', swap))  3.52 us
    ppermute x4, waiting for transfers between devices, keep(): hops[p].append(lax.ppermute(grad, 'pipe', hop))  2.15 us
  transfers between devices with their start and end apart: 20, of which 7 were waited for; matrix products, arithmetic and copies ran while one was open for 0% of the time, Pallas kernels for 11%

commit v1 on v0

--- a/solution.py
+++ b/solution.py
@@ -112,8 +112,6 @@
     twice = (row == col % rank).astype(BF16)
     order = rank + jnp.where(row < rank // 2, 2 * row, 2 * row - rank + 1)
     split = jnp.logical_and(col == order, row < rank).astype(BF16)
-    mix_act[k, :, :, head_size:] = jnp.zeros((heads, head_size, both), BF16)
-    mix_grad[k, :, head_size:, :] = jnp.zeros((heads, both, head_size), BF16)
     for j in range(picks):
         own = blocks[k, 0, j] - first_head
 
@@ -156,6 +154,9 @@
     left = micro - 2 * chunk
     rest = [load(acts.at[k, pl.ds(2 * chunk, left)], acts_v.at[k, pl.ds(2 * chunk, left)]) for k in order]
     rest.append(load(top.at[pl.ds(chunk, micro - chunk)], top_v.at[pl.ds(chunk, micro - chunk)]))
+    for k in order:
+        mix_act[k, :, :, head_size:] = jnp.zeros((*mix_act.shape[1:3], mix_act.shape[3] - head_size), BF16)
+        mix_grad[k, :, head_size:, :] = jnp.zeros((mix_grad.shape[1], mix_grad.shape[2] - head_size, head_size), BF16)
     for copy in scalars:
         copy.wait()
     live = sizes[lax.axis_index("pipe")]
@@ -167,7 +168,7 @@
         for copy in need[k]:
             copy.wait()
         pl.when(k < live)(functools.partial(slopes_of, k, 0, acts_v, mix_act, slopes, part))
-    for copy in first + second:
+    for copy in first:
         copy.wait()
     active, odd = here(pair)
     ahead = jnp.logical_and(active, odd)
@@ -176,6 +177,8 @@
     def _():
         chain(live, top_v[:chunk], slopes, mix_grad, grad, proj)
 
+    for copy in second:
+        copy.wait()
     for k in order:
         pl.when(jnp.logical_and(k < live, jnp.logical_not(ahead)))(
             functools.partial(slopes_of, k, chunk, acts_v, mix_act, next_slopes, next_part)

time: 51.2 us -> 52.4 us (1.023)
  starting transfers between devices: 25.8 us -> 26.9 us
  waiting for transfers between devices: 14.7 us -> 15.3 us
    ppermute x8, starting transfers between devices: 3.52 us -> 7.27 us  [keep(): core[p].append(lax.ppermute(grad, 'pipe', swap))]
    ppermute x4, starting transfers between devices: 9.11 us -> 6.97 us  [keep(): hops[p].append(lax.ppermute(grad, 'pipe', hop))]
    ppermute x8, waiting for transfers between devices: 11.9 us -> 13.8 us  [exchange(): lax.ppermute(x, axis, [(i, i ^ by) for i in range(lax.axis_size(axis))])]
    ppermute x4, waiting for transfers between devices: 2.15 us -> 0.81 us  [keep(): hops[p].append(lax.ppermute(grad, 'pipe', hop))]
  transfers between devices with their start and end apart: 20 -> 20, of which waited for: 7 -> 9; matrix products, arithmetic and copies ran while one was open for 0% -> 0% of each run, Pallas kernels for 11% -> 10%
where the time goes in v1:
time: 52.4 us; the launch traced here: 52.5 us
  starting transfers between devices  26.9 us (51%)
  waiting for transfers between devices  15.3 us (29%)
  Pallas kernels  9.45 us (18%)
  between operations  0.83 us (2%)
    ppermute x8, waiting for transfers between devices, exchange(): lax.ppermute(x, axis, [(i, i ^ by) for i in range(lax.axis_size(axis))])  13.8 us
    ppermute x8, starting transfers between devices, exchange(): lax.ppermute(x, axis, [(i, i ^ by) for i in range(lax.axis_size(axis))])  12.7 us
    pallas_call x26, Pallas kernels, call(): pl.pallas_call(kernel, out_shape=outs, in_specs=specs, out_specs=(VMEM,)...  9.45 us
    ppermute x8, starting transfers between devices, keep(): core[p].append(lax.ppermute(grad, 'pipe', swap))  7.27 us
    ppermute x4, starting transfers between devices, keep(): hops[p].append(lax.ppermute(grad, 'pipe', hop))  6.97 us
  transfers between devices with their start and end apart: 20, of which 9 were waited for; matrix products, arithmetic and copies ran while one was open for 0% of the time, Pallas kernels for 10%

profile of v1, /device:TPU:0, one launch (start us, length us, event | category | flops | bytes accessed | tf_op | source)
XLA Modules:
  0.0 52.5 jit_solution(848030008896236100)
XLA Ops:
  0.6 3.1 %first.1 = (bf16[2,64,1024]{2,1,0:T(8,128)(2,1)S(1)}, bf16[3,128,128]{2,1,0:T(8,128)(2,1)S(1)}, f32[3,2,64,1024]{3,2,1,0:T(8,128)S(1)}, bf16[3,128,128]{2,1,0:T(...) custom-call(s32[4]{0:T(128)} %sizes_in.1, ...), custom_call_target="tpu_custom_call" | custom-call | flops 1000 | bytes 1000 | tf_op jit(solution)/shard_map/first/pallas_call | solution.py:374
  3.7 1.5 %collective-permute-start.1 = (bf16[2,64,1024]{2,1,0:T(8,128)(2,1)S(1)}, bf16[2,64,1024]{2,1,0:T(8,128)(2,1)S(1)}, u32[]{:S(2)}, u32[]{:S(2)}) collective-permute-start(bf16[2,64,1024]{2,1,0:T(8,128)(2,1)S(1)} %get-tuple-element.82.refs_0_), channel_id=1, source_target_pairs={{0,4},{4,0},{8,12},{12,8},{1,5},{5,1},{9,13},{13,9},{2,6},{6,2},{1... | collective-permute-start | bytes 786440 | tf_op jit(solution)/shard_map/ppermute | solution.py:438
  5.3 0.5 beside.1
  5.8 0.6 %collective-permute-done.1.even_in = bf16[2,64,1024]{2,1,0:T(8,128)(2,1)S(1)} collective-permute-done((bf16[2,64,1024]{2,1,0:T(8,128)(2,1)S(1)}, bf16[2,64,1024]{2,1,0:T(8,128)(2,1)S(1)}, u32[]{:S(2)}, u32[]{:S(2)}) %collective-permute-start.1) | collective-permute-done | bytes 262176 | tf_op jit(solution)/shard_map/ppermute | solution.py:438
  6.4 0.4 collective-permute-start.2
  6.8 2.6 %collective-permute-start = (bf16[2,3,128,128]{3,2,1,0:T(8,128)(2,1)S(1)}, bf16[2,3,128,128]{3,2,1,0:T(8,128)(2,1)S(1)}, u32[]{:S(2)}, u32[]{:S(2)}) collective-permute-start(bf16[2,3,128,128]{3,2,1,0:T(8,128)(2,1)S(1)} %get-tuple-element.79.mine), channel_id=1, source_target_pairs={{0,1},{1,0},{2,3},{3,2},{4,5},{5,4},{6,7},{7,6},{8,9},{9,8},{10,11... | collective-permute-start | bytes 589832 | tf_op jit(solution)/shard_map/ppermute | solution.py:352
  9.4 0.7 %collective-permute-start.5 = (bf16[2,64,1024]{2,1,0:T(8,128)(2,1)S(1)}, bf16[2,64,1024]{2,1,0:T(8,128)(2,1)S(1)}, u32[]{:S(2)}, u32[]{:S(2)}) collective-permute-start(bf16[2,64,1024]{2,1,0:T(8,128)(2,1)S(1)} %get-tuple-element.86.refs_1_.refs_4_), channel_id=1, source_target_pairs={{8,4},{9,5},{10,6},{11,7},{24,20},{25,21},{26,22},{27,23}} | collective-permute-start | bytes 786440 | tf_op jit(solution)/shard_map/ppermute | solution.py:444
  10.0 0.0 collective-permute-done.2.even_in
  10.1 0.5 %collective-permute-start.4 = (bf16[2,64,1024]{2,1,0:T(8,128)(2,1)S(1)}, bf16[2,64,1024]{2,1,0:T(8,128)(2,1)S(1)}, u32[]{:S(2)}, u32[]{:S(2)}) collective-permute-start(bf16[2,64,1024]{2,1,0:T(8,128)(2,1)S(1)} %get-tuple-element.92.refs_2_.refs_5_), channel_id=1, source_target_pairs={{0,4},{4,0},{8,12},{12,8},{1,5},{5,1},{9,13},{13,9},{2,6},{6,2},{1... | collective-permute-start | bytes 786440 | tf_op jit(solution)/shard_map/ppermute | solution.py:438
  10.6 0.7 %collective-permute-start.7 = (bf16[2,64,1024]{2,1,0:T(8,128)(2,1)S(1)}, bf16[2,64,1024]{2,1,0:T(8,128)(2,1)S(1)}, u32[]{:S(2)}, u32[]{:S(2)}) collective-permute-start(bf16[2,64,1024]{2,1,0:T(8,128)(2,1)S(1)} %get-tuple-element.92.refs_2_.refs_5_), channel_id=1, source_target_pairs={{8,4},{9,5},{10,6},{11,7},{24,20},{25,21},{26,22},{27,23}} | collective-permute-start | bytes 786440 | tf_op jit(solution)/shard_map/ppermute | solution.py:444
  11.3 0.4 slope.1
  11.7 2.8 %collective-permute-done.other = bf16[2,3,128,128]{3,2,1,0:T(8,128)(2,1)S(1)} collective-permute-done((bf16[2,3,128,128]{3,2,1,0:T(8,128)(2,1)S(1)}, bf16[2,3,128,128]{3,2,1,0:T(8,128)(2,1)S(1)}, u32[]{:S(2)}, u32[]{:S(2)}) %collective-permute-start) | collective-permute-done | bytes 196640 | tf_op jit(solution)/shard_map/ppermute | solution.py:352
  14.6 3.0 %collective-permute-start.3 = (bf16[2,3,128,128]{3,2,1,0:T(8,128)(2,1)S(1)}, bf16[2,3,128,128]{3,2,1,0:T(8,128)(2,1)S(1)}, u32[]{:S(2)}, u32[]{:S(2)}) collective-permute-start(bf16[2,3,128,128]{3,2,1,0:T(8,128)(2,1)S(1)} %get-tuple-element.90.mine), channel_id=1, source_target_pairs={{0,2},{1,3},{2,0},{3,1},{4,6},{5,7},{6,4},{7,5},{8,10},{9,11},{10,... | collective-permute-start | bytes 589832 | tf_op jit(solution)/shard_map/ppermute | solution.py:352
  17.6 0.0 collective-permute-done.4.even_in
  17.6 4.6 %collective-permute-start.10 = (bf16[2,64,1024]{2,1,0:T(8,128)(2,1)S(1)}, bf16[2,64,1024]{2,1,0:T(8,128)(2,1)S(1)}, u32[]{:S(2)}, u32[]{:S(2)}) collective-permute-start(bf16[2,64,1024]{2,1,0:T(8,128)(2,1)S(1)} %get-tuple-element.96.refs_3_.refs_6_), channel_id=1, source_target_pairs={{0,12},{4,0},{8,4},{12,8},{1,13},{5,1},{9,5},{13,9},{2,14},{6,2},{... | collective-permute-start | bytes 786440 | tf_op jit(solution)/shard_map/ppermute | solution.py:444
  22.2 0.0 collective-permute-start.8
  22.2 0.0 collective-permute-done.6.even_in
  22.3 0.2 step.9
  22.5 1.6 %collective-permute-start.9 = (bf16[2,64,1024]{2,1,0:T(8,128)(2,1)S(1)}, bf16[2,64,1024]{2,1,0:T(8,128)(2,1)S(1)}, u32[]{:S(2)}, u32[]{:S(2)}) collective-permute-start(bf16[2,64,1024]{2,1,0:T(8,128)(2,1)S(1)} %get-tuple-element.102.refs_9_), channel_id=1, source_target_pairs={{0,4},{4,0},{8,12},{12,8},{1,5},{5,1},{9,13},{13,9},{2,6},{6,2},{1... | collective-permute-start | bytes 786440 | tf_op jit(solution)/shard_map/ppermute | solution.py:438
  24.0 1.0 %collective-permute-start.11 = (bf16[2,64,1024]{2,1,0:T(8,128)(2,1)S(1)}, bf16[2,64,1024]{2,1,0:T(8,128)(2,1)S(1)}, u32[]{:S(2)}, u32[]{:S(2)}) collective-permute-start(bf16[2,64,1024]{2,1,0:T(8,128)(2,1)S(1)} %get-tuple-element.115.refs_7_), channel_id=1, source_target_pairs={{0,12},{4,0},{8,4},{12,8},{1,13},{5,1},{9,5},{13,9},{2,14},{6,2},{... | collective-permute-start | bytes 786440 | tf_op jit(solution)/shard_map/ppermute | solution.py:444
  25.1 0.0 collective-permute-done.8.source
  25.1 0.4 step.10
  25.5 0.0 collective-permute-done.9.source
  25.5 0.4 step.11
  26.0 0.3 collective-permute-done.3.other
  26.2 0.1 widen.2
  26.3 0.5 %sketch.2 = (bf16[3,4,32,128]{3,2,1,0:T(8,128)(2,1)S(1)}, f32[8,128]{1,0:T(8,128)S(1)}) custom-call(f32[8,128]{1,0:T(8,128)S(1)} %get-tuple-element.74.info.after, f32[8,128]{1,0:T(8,128)S(1)} %get-tuple-element.104.after, bf16[3,128,128]{2,1,0:T(8,128)(2,1)S(1)} %get-tuple-element.105.refs_0_, bf16[3,128,128]{2,1,0:T(8,128)(2,1)S(1)} %get-tuple-element.106.refs_1_.refs_2_, ...), custom_call_target="tpu_custom_call" | custom-call | flops 2000000000 | bytes 1000 | tf_op jit(solution)/shard_map/sketch/pallas_call | solution.py:374
  26.9 1.2 %collective-permute-start.12 = (bf16[2,64,1024]{2,1,0:T(8,128)(2,1)S(1)}, bf16[2,64,1024]{2,1,0:T(8,128)(2,1)S(1)}, u32[]{:S(2)}, u32[]{:S(2)}) collective-permute-start(bf16[2,64,1024]{2,1,0:T(8,128)(2,1)S(1)} %get-tuple-element.117.refs_10_), channel_id=1, source_target_pairs={{0,4},{4,0},{8,12},{12,8},{1,5},{5,1},{9,13},{13,9},{2,6},{6,2},{1... | collective-permute-start | bytes 786440 | tf_op jit(solution)/shard_map/ppermute | solution.py:438
  28.2 0.8 %collective-permute-done.11.source = bf16[2,64,1024]{2,1,0:T(8,128)(2,1)S(1)} collective-permute-done((bf16[2,64,1024]{2,1,0:T(8,128)(2,1)S(1)}, bf16[2,64,1024]{2,1,0:T(8,128)(2,1)S(1)}, u32[]{:S(2)}, u32[]{:S(2)}) %collective-permute-start.11) | collective-permute-done | bytes 262176 | tf_op jit(solution)/shard_map/ppermute | solution.py:444
  29.0 2.0 %collective-permute-start.13 = (bf16[2,64,1024]{2,1,0:T(8,128)(2,1)S(1)}, bf16[2,64,1024]{2,1,0:T(8,128)(2,1)S(1)}, u32[]{:S(2)}, u32[]{:S(2)}) collective-permute-start(bf16[2,64,1024]{2,1,0:T(8,128)(2,1)S(1)} %get-tuple-element.119.refs_11_), channel_id=1, source_target_pairs={{0,4},{4,0},{8,12},{12,8},{1,5},{5,1},{9,13},{13,9},{2,6},{6,2},{1... | collective-permute-start | bytes 786440 | tf_op jit(solution)/shard_map/ppermute | solution.py:438
  31.0 0.9 %collective-permute-start.15 = (bf16[3,4,32,128]{3,2,1,0:T(8,128)(2,1)S(1)}, bf16[3,4,32,128]{3,2,1,0:T(8,128)(2,1)S(1)}, u32[]{:S(2)}, u32[]{:S(2)}) collective-permute-start(bf16[3,4,32,128]{3,2,1,0:T(8,128)(2,1)S(1)} %get-tuple-element.130.mine), channel_id=1, source_target_pairs={{0,1},{1,0},{2,3},{3,2},{4,5},{5,4},{6,7},{7,6},{8,9},{9,8},{10,11... | collective-permute-start | bytes 294920 | tf_op jit(solution)/shard_map/ppermute | solution.py:352
  32.0 0.4 step.14
  32.4 0.4 step.15
  32.9 0.1 widen.3
  33.0 0.5 %sketch.3 = (bf16[3,4,32,128]{3,2,1,0:T(8,128)(2,1)S(1)}, f32[8,128]{1,0:T(8,128)S(1)}) custom-call(f32[8,128]{1,0:T(8,128)S(1)} %get-tuple-element.74.info.after, f32[8,128]{1,0:T(8,128)S(1)} %get-tuple-element.121.after, bf16[3,128,128]{2,1,0:T(8,128)(2,1)S(1)} %get-tuple-element.107.refs_3_.refs_0_, ...), custom_call_target="tpu_custom_call" | custom-call | flops 1000000 | bytes 1000 | tf_op jit(solution)/shard_map/sketch/pallas_call | solution.py:374
  33.5 1.6 %collective-permute-start.14 = (bf16[3,4,32,128]{3,2,1,0:T(8,128)(2,1)S(1)}, bf16[3,4,32,128]{3,2,1,0:T(8,128)(2,1)S(1)}, u32[]{:S(2)}, u32[]{:S(2)}) collective-permute-start(bf16[3,4,32,128]{3,2,1,0:T(8,128)(2,1)S(1)} %get-tuple-element.129.mine), channel_id=1, source_target_pairs={{0,16},{16,0},{1,17},{17,1},{2,18},{18,2},{3,19},{19,3},{4,20},{20... | collective-permute-start | bytes 294920 | tf_op jit(solution)/shard_map/ppermute | solution.py:352
  35.1 0.7 %collective-permute-done.15.other = bf16[3,4,32,128]{3,2,1,0:T(8,128)(2,1)S(1)} collective-permute-done((bf16[3,4,32,128]{3,2,1,0:T(8,128)(2,1)S(1)}, bf16[3,4,32,128]{3,2,1,0:T(8,128)(2,1)S(1)}, u32[]{:S(2)}, u32[]{:S(2)}) %collective-permute-start.15) | collective-permute-done | bytes 98336 | tf_op jit(solution)/shard_map/ppermute | solution.py:352
  35.8 1.4 %collective-permute-start.17 = (bf16[3,4,32,128]{3,2,1,0:T(8,128)(2,1)S(1)}, bf16[3,4,32,128]{3,2,1,0:T(8,128)(2,1)S(1)}, u32[]{:S(2)}, u32[]{:S(2)}) collective-permute-start(bf16[3,4,32,128]{3,2,1,0:T(8,128)(2,1)S(1)} %get-tuple-element.140.mine), channel_id=1, source_target_pairs={{0,2},{1,3},{2,0},{3,1},{4,6},{5,7},{6,4},{7,5},{8,10},{9,11},{10,... | collective-permute-start | bytes 294920 | tf_op jit(solution)/shard_map/ppermute | solution.py:352
  37.2 1.6 %collective-permute-done.14.other = bf16[3,4,32,128]{3,2,1,0:T(8,128)(2,1)S(1)} collective-permute-done((bf16[3,4,32,128]{3,2,1,0:T(8,128)(2,1)S(1)}, bf16[3,4,32,128]{3,2,1,0:T(8,128)(2,1)S(1)}, u32[]{:S(2)}, u32[]{:S(2)}) %collective-permute-start.14) | collective-permute-done | bytes 98336 | tf_op jit(solution)/shard_map/ppermute | solution.py:352
  38.8 1.0 %collective-permute-start.16 = (bf16[3,4,32,128]{3,2,1,0:T(8,128)(2,1)S(1)}, bf16[3,4,32,128]{3,2,1,0:T(8,128)(2,1)S(1)}, u32[]{:S(2)}, u32[]{:S(2)}) collective-permute-start(bf16[3,4,32,128]{3,2,1,0:T(8,128)(2,1)S(1)} %get-tuple-element.139.mine), channel_id=1, source_target_pairs={{0,1},{1,0},{2,3},{3,2},{4,5},{5,4},{6,7},{7,6},{8,9},{9,8},{10,11... | collective-permute-start | bytes 294920 | tf_op jit(solution)/shard_map/ppermute | solution.py:352
  39.8 1.0 %collect.1 = (bf16[8,64,1024]{2,1,0:T(8,128)(2,1)}, f32[8,128]{1,0:T(8,128)S(1)}) custom-call(f32[8,128]{1,0:T(8,128)S(1)} %get-tuple-element.133.after, bf16[2,64,1024]{2,1,0:T(8,128)(2,1)S(1)} %get-tuple-element.82.refs_0_, bf16[2,64,1024]{2,1,0:T(8,128)(2,1)S(1)} %get-tuple-element.86.refs_1_.refs_4_, ...), custom_call_target="tpu_custom_call" | custom-call | flops 10000000000 | bytes 1000 | tf_op jit(solution)/shard_map/collect/pallas_call | solution.py:374
  40.8 2.3 %collective-permute-done.17.other = bf16[3,4,32,128]{3,2,1,0:T(8,128)(2,1)S(1)} collective-permute-done((bf16[3,4,32,128]{3,2,1,0:T(8,128)(2,1)S(1)}, bf16[3,4,32,128]{3,2,1,0:T(8,128)(2,1)S(1)}, u32[]{:S(2)}, u32[]{:S(2)}) %collective-permute-start.17) | collective-permute-done | bytes 98336 | tf_op jit(solution)/shard_map/ppermute | solution.py:352
  43.2 1.3 %collective-permute-start.18 = (bf16[3,4,32,128]{3,2,1,0:T(8,128)(2,1)S(1)}, bf16[3,4,32,128]{3,2,1,0:T(8,128)(2,1)S(1)}, u32[]{:S(2)}, u32[]{:S(2)}) collective-permute-start(bf16[3,4,32,128]{3,2,1,0:T(8,128)(2,1)S(1)} %get-tuple-element.144.refs_0_), channel_id=1, source_target_pairs={{0,16},{16,0},{1,17},{17,1},{2,18},{18,2},{3,19},{19,3},{4,20},{20... | collective-permute-start | bytes 294920 | tf_op jit(solution)/shard_map/ppermute | solution.py:352
  44.5 0.0 collective-permute-done.16.other
  44.6 1.0 %collective-permute-start.19 = (bf16[3,4,32,128]{3,2,1,0:T(8,128)(2,1)S(1)}, bf16[3,4,32,128]{3,2,1,0:T(8,128)(2,1)S(1)}, u32[]{:S(2)}, u32[]{:S(2)}) collective-permute-start(bf16[3,4,32,128]{3,2,1,0:T(8,128)(2,1)S(1)} %get-tuple-element.145.refs_2_), channel_id=1, source_target_pairs={{0,2},{1,3},{2,0},{3,1},{4,6},{5,7},{6,4},{7,5},{8,10},{9,11},{10,... | collective-permute-start | bytes 294920 | tf_op jit(solution)/shard_map/ppermute | solution.py:352
  45.5 2.3 %collective-permute-done.18.refs_1_ = bf16[3,4,32,128]{3,2,1,0:T(8,128)(2,1)S(1)} collective-permute-done((bf16[3,4,32,128]{3,2,1,0:T(8,128)(2,1)S(1)}, bf16[3,4,32,128]{3,2,1,0:T(8,128)(2,1)S(1)}, u32[]{:S(2)}, u32[]{:S(2)}) %collective-permute-start.18) | collective-permute-done | bytes 98336 | tf_op jit(solution)/shard_map/ppermute | solution.py:352
  47.9 3.8 %collective-permute-done.19.refs_3_ = bf16[3,4,32,128]{3,2,1,0:T(8,128)(2,1)S(1)} collective-permute-done((bf16[3,4,32,128]{3,2,1,0:T(8,128)(2,1)S(1)}, bf16[3,4,32,128]{3,2,1,0:T(8,128)(2,1)S(1)}, u32[]{:S(2)}, u32[]{:S(2)}) %collective-permute-start.19) | collective-permute-done | bytes 98336 | tf_op jit(solution)/shard_map/ppermute | solution.py:352
  51.6 0.9 %last.1 = f32[3,8,4096]{2,1,0:T(8,128)} custom-call(f32[8,128]{1,0:T(8,128)S(1)} %get-tuple-element.143.after, bf16[3,4,32,128]{3,2,1,0:T(8,128)(2,1)S(1)} %get-tuple-element.144.refs_0_, bf16[3,4,32,128]{3,2,1,0:T(8,128)(2,1)S(1)} %collective-permute-done.18.refs_1_, bf16[3,4,32,128]{3,2,1,0:T(8,128)(2,1)S(1)} %get-tuple-element.145.refs_2_, ...), custom_call_target="tpu_custom_call" | custom-call | flops 1000 | bytes 1000 | tf_op jit(solution)/shard_map/last/pallas_call | solution.py:374
  (18 shorter events, 0.3 us)
Async XLA Ops:
  3.7 2.7 %collective-permute-start.1 = (bf16[2,64,1024]{2,1,0:T(8,128)(2,1)S(1)}, bf16[2,64,1024]{2,1,0:T(8,128)(2,1)S(1)}, u32[]{:S(2)}, u32[]{:S(2)}) collective-permute-start(bf16[2,64,1024]{2,1,0:T(8,128)(2,1)S(1)} %get-tuple-element.82.refs_0_), channel_id=1, source_target_pairs={{0,4},{4,0},{8,12},{12,8},{1,5},{5,1},{9,13},{13,9},{2,6},{6,2},{1... | collective-permute-start | bytes 786440 | tf_op jit(solution)/shard_map/ppermute | solution.py:438
  6.4 3.6 %collective-permute-start.2 = (bf16[2,64,1024]{2,1,0:T(8,128)(2,1)S(1)}, bf16[2,64,1024]{2,1,0:T(8,128)(2,1)S(1)}, u32[]{:S(2)}, u32[]{:S(2)}) collective-permute-start(bf16[2,64,1024]{2,1,0:T(8,128)(2,1)S(1)} %get-tuple-element.86.refs_1_.refs_4_), channel_id=1, source_target_pairs={{0,4},{4,0},{8,12},{12,8},{1,5},{5,1},{9,13},{13,9},{2,6},{6,2},{1... | collective-permute-start | bytes 786440 | tf_op jit(solution)/shard_map/ppermute | solution.py:438
  6.8 7.8 %collective-permute-start = (bf16[2,3,128,128]{3,2,1,0:T(8,128)(2,1)S(1)}, bf16[2,3,128,128]{3,2,1,0:T(8,128)(2,1)S(1)}, u32[]{:S(2)}, u32[]{:S(2)}) collective-permute-start(bf16[2,3,128,128]{3,2,1,0:T(8,128)(2,1)S(1)} %get-tuple-element.79.mine), channel_id=1, source_target_pairs={{0,1},{1,0},{2,3},{3,2},{4,5},{5,4},{6,7},{7,6},{8,9},{9,8},{10,11... | collective-permute-start | bytes 589832 | tf_op jit(solution)/shard_map/ppermute | solution.py:352
  9.4 12.8 %collective-permute-start.5 = (bf16[2,64,1024]{2,1,0:T(8,128)(2,1)S(1)}, bf16[2,64,1024]{2,1,0:T(8,128)(2,1)S(1)}, u32[]{:S(2)}, u32[]{:S(2)}) collective-permute-start(bf16[2,64,1024]{2,1,0:T(8,128)(2,1)S(1)} %get-tuple-element.86.refs_1_.refs_4_), channel_id=1, source_target_pairs={{8,4},{9,5},{10,6},{11,7},{24,20},{25,21},{26,22},{27,23}} | collective-permute-start | bytes 786440 | tf_op jit(solution)/shard_map/ppermute | solution.py:444
  10.1 7.5 %collective-permute-start.4 = (bf16[2,64,1024]{2,1,0:T(8,128)(2,1)S(1)}, bf16[2,64,1024]{2,1,0:T(8,128)(2,1)S(1)}, u32[]{:S(2)}, u32[]{:S(2)}) collective-permute-start(bf16[2,64,1024]{2,1,0:T(8,128)(2,1)S(1)} %get-tuple-element.92.refs_2_.refs_5_), channel_id=1, source_target_pairs={{0,4},{4,0},{8,12},{12,8},{1,5},{5,1},{9,13},{13,9},{2,6},{6,2},{1... | collective-permute-start | bytes 786440 | tf_op jit(solution)/shard_map/ppermute | solution.py:438
  10.6 11.6 %collective-permute-start.7 = (bf16[2,64,1024]{2,1,0:T(8,128)(2,1)S(1)}, bf16[2,64,1024]{2,1,0:T(8,128)(2,1)S(1)}, u32[]{:S(2)}, u32[]{:S(2)}) collective-permute-start(bf16[2,64,1024]{2,1,0:T(8,128)(2,1)S(1)} %get-tuple-element.92.refs_2_.refs_5_), channel_id=1, source_target_pairs={{8,4},{9,5},{10,6},{11,7},{24,20},{25,21},{26,22},{27,23}} | collective-permute-start | bytes 786440 | tf_op jit(solution)/shard_map/ppermute | solution.py:444
  14.6 11.6 %collective-permute-start.3 = (bf16[2,3,128,128]{3,2,1,0:T(8,128)(2,1)S(1)}, bf16[2,3,128,128]{3,2,1,0:T(8,128)(2,1)S(1)}, u32[]{:S(2)}, u32[]{:S(2)}) collective-permute-start(bf16[2,3,128,128]{3,2,1,0:T(8,128)(2,1)S(1)} %get-tuple-element.90.mine), channel_id=1, source_target_pairs={{0,2},{1,3},{2,0},{3,1},{4,6},{5,7},{6,4},{7,5},{8,10},{9,11},{10,... | collective-permute-start | bytes 589832 | tf_op jit(solution)/shard_map/ppermute | solution.py:352
  17.6 4.6 %collective-permute-start.6 = (bf16[2,64,1024]{2,1,0:T(8,128)(2,1)S(1)}, bf16[2,64,1024]{2,1,0:T(8,128)(2,1)S(1)}, u32[]{:S(2)}, u32[]{:S(2)}) collective-permute-start(bf16[2,64,1024]{2,1,0:T(8,128)(2,1)S(1)} %get-tuple-element.96.refs_3_.refs_6_), channel_id=1, source_target_pairs={{0,4},{4,0},{8,12},{12,8},{1,5},{5,1},{9,13},{13,9},{2,6},{6,2},{1... | collective-permute-start | bytes 786440 | tf_op jit(solution)/shard_map/ppermute | solution.py:438
  17.6 9.3 %collective-permute-start.10 = (bf16[2,64,1024]{2,1,0:T(8,128)(2,1)S(1)}, bf16[2,64,1024]{2,1,0:T(8,128)(2,1)S(1)}, u32[]{:S(2)}, u32[]{:S(2)}) collective-permute-start(bf16[2,64,1024]{2,1,0:T(8,128)(2,1)S(1)} %get-tuple-element.96.refs_3_.refs_6_), channel_id=1, source_target_pairs={{0,12},{4,0},{8,4},{12,8},{1,13},{5,1},{9,5},{13,9},{2,14},{6,2},{... | collective-permute-start | bytes 786440 | tf_op jit(solution)/shard_map/ppermute | solution.py:444
  22.2 2.9 %collective-permute-start.8 = (bf16[2,64,1024]{2,1,0:T(8,128)(2,1)S(1)}, bf16[2,64,1024]{2,1,0:T(8,128)(2,1)S(1)}, u32[]{:S(2)}, u32[]{:S(2)}) collective-permute-start(bf16[2,64,1024]{2,1,0:T(8,128)(2,1)S(1)} %get-tuple-element.100.refs_8_), channel_id=1, source_target_pairs={{0,4},{4,0},{8,12},{12,8},{1,5},{5,1},{9,13},{13,9},{2,6},{6,2},{1... | collective-permute-start | bytes 786440 | tf_op jit(solution)/shard_map/ppermute | solution.py:438
  22.5 3.0 %collective-permute-start.9 = (bf16[2,64,1024]{2,1,0:T(8,128)(2,1)S(1)}, bf16[2,64,1024]{2,1,0:T(8,128)(2,1)S(1)}, u32[]{:S(2)}, u32[]{:S(2)}) collective-permute-start(bf16[2,64,1024]{2,1,0:T(8,128)(2,1)S(1)} %get-tuple-element.102.refs_9_), channel_id=1, source_target_pairs={{0,4},{4,0},{8,12},{12,8},{1,5},{5,1},{9,13},{13,9},{2,6},{6,2},{1... | collective-permute-start | bytes 786440 | tf_op jit(solution)/shard_map/ppermute | solution.py:438
  24.0 4.9 %collective-permute-start.11 = (bf16[2,64,1024]{2,1,0:T(8,128)(2,1)S(1)}, bf16[2,64,1024]{2,1,0:T(8,128)(2,1)S(1)}, u32[]{:S(2)}, u32[]{:S(2)}) collective-permute-start(bf16[2,64,1024]{2,1,0:T(8,128)(2,1)S(1)} %get-tuple-element.115.refs_7_), channel_id=1, source_target_pairs={{0,12},{4,0},{8,4},{12,8},{1,13},{5,1},{9,5},{13,9},{2,14},{6,2},{... | collective-permute-start | bytes 786440 | tf_op jit(solution)/shard_map/ppermute | solution.py:444
  26.9 5.0 %collective-permute-start.12 = (bf16[2,64,1024]{2,1,0:T(8,128)(2,1)S(1)}, bf16[2,64,1024]{2,1,0:T(8,128)(2,1)S(1)}, u32[]{:S(2)}, u32[]{:S(2)}) collective-permute-start(bf16[2,64,1024]{2,1,0:T(8,128)(2,1)S(1)} %get-tuple-element.117.refs_10_), channel_id=1, source_target_pairs={{0,4},{4,0},{8,12},{12,8},{1,5},{5,1},{9,13},{13,9},{2,6},{6,2},{1... | collective-permute-start | bytes 786440 | tf_op jit(solution)/shard_map/ppermute | solution.py:438
  29.0 3.4 %collective-permute-start.13 = (bf16[2,64,1024]{2,1,0:T(8,128)(2,1)S(1)}, bf16[2,64,1024]{2,1,0:T(8,128)(2,1)S(1)}, u32[]{:S(2)}, u32[]{:S(2)}) collective-permute-start(bf16[2,64,1024]{2,1,0:T(8,128)(2,1)S(1)} %get-tuple-element.119.refs_11_), channel_id=1, source_target_pairs={{0,4},{4,0},{8,12},{12,8},{1,5},{5,1},{9,13},{13,9},{2,6},{6,2},{1... | collective-permute-start | bytes 786440 | tf_op jit(solution)/shard_map/ppermute | solution.py:438
  31.0 4.8 %collective-permute-start.15 = (bf16[3,4,32,128]{3,2,1,0:T(8,128)(2,1)S(1)}, bf16[3,4,32,128]{3,2,1,0:T(8,128)(2,1)S(1)}, u32[]{:S(2)}, u32[]{:S(2)}) collective-permute-start(bf16[3,4,32,128]{3,2,1,0:T(8,128)(2,1)S(1)} %get-tuple-element.130.mine), channel_id=1, source_target_pairs={{0,1},{1,0},{2,3},{3,2},{4,5},{5,4},{6,7},{7,6},{8,9},{9,8},{10,11... | collective-permute-start | bytes 294920 | tf_op jit(solution)/shard_map/ppermute | solution.py:352
  33.5 5.2 %collective-permute-start.14 = (bf16[3,4,32,128]{3,2,1,0:T(8,128)(2,1)S(1)}, bf16[3,4,32,128]{3,2,1,0:T(8,128)(2,1)S(1)}, u32[]{:S(2)}, u32[]{:S(2)}) collective-permute-start(bf16[3,4,32,128]{3,2,1,0:T(8,128)(2,1)S(1)} %get-tuple-element.129.mine), channel_id=1, source_target_pairs={{0,16},{16,0},{1,17},{17,1},{2,18},{18,2},{3,19},{19,3},{4,20},{20... | collective-permute-start | bytes 294920 | tf_op jit(solution)/shard_map/ppermute | solution.py:352
  35.8 7.3 %collective-permute-start.17 = (bf16[3,4,32,128]{3,2,1,0:T(8,128)(2,1)S(1)}, bf16[3,4,32,128]{3,2,1,0:T(8,128)(2,1)S(1)}, u32[]{:S(2)}, u32[]{:S(2)}) collective-permute-start(bf16[3,4,32,128]{3,2,1,0:T(8,128)(2,1)S(1)} %get-tuple-element.140.mine), channel_id=1, source_target_pairs={{0,2},{1,3},{2,0},{3,1},{4,6},{5,7},{6,4},{7,5},{8,10},{9,11},{10,... | collective-permute-start | bytes 294920 | tf_op jit(solution)/shard_map/ppermute | solution.py:352
  38.8 5.7 %collective-permute-start.16 = (bf16[3,4,32,128]{3,2,1,0:T(8,128)(2,1)S(1)}, bf16[3,4,32,128]{3,2,1,0:T(8,128)(2,1)S(1)}, u32[]{:S(2)}, u32[]{:S(2)}) collective-permute-start(bf16[3,4,32,128]{3,2,1,0:T(8,128)(2,1)S(1)} %get-tuple-element.139.mine), channel_id=1, source_target_pairs={{0,1},{1,0},{2,3},{3,2},{4,5},{5,4},{6,7},{7,6},{8,9},{9,8},{10,11... | collective-permute-start | bytes 294920 | tf_op jit(solution)/shard_map/ppermute | solution.py:352
  43.2 4.7 %collective-permute-start.18 = (bf16[3,4,32,128]{3,2,1,0:T(8,128)(2,1)S(1)}, bf16[3,4,32,128]{3,2,1,0:T(8,128)(2,1)S(1)}, u32[]{:S(2)}, u32[]{:S(2)}) collective-permute-start(bf16[3,4,32,128]{3,2,1,0:T(8,128)(2,1)S(1)} %get-tuple-element.144.refs_0_), channel_id=1, source_target_pairs={{0,16},{16,0},{1,17},{17,1},{2,18},{18,2},{3,19},{19,3},{4,20},{20... | collective-permute-start | bytes 294920 | tf_op jit(solution)/shard_map/ppermute | solution.py:352
  44.6 7.1 %collective-permute-start.19 = (bf16[3,4,32,128]{3,2,1,0:T(8,128)(2,1)S(1)}, bf16[3,4,32,128]{3,2,1,0:T(8,128)(2,1)S(1)}, u32[]{:S(2)}, u32[]{:S(2)}) collective-permute-start(bf16[3,4,32,128]{3,2,1,0:T(8,128)(2,1)S(1)} %get-tuple-element.145.refs_2_), channel_id=1, source_target_pairs={{0,2},{1,3},{2,0},{3,1},{4,6},{5,7},{6,4},{7,5},{8,10},{9,11},{10,... | collective-permute-start | bytes 294920 | tf_op jit(solution)/shard_map/ppermute | solution.py:352

commit v2 on v0

--- a/solution.py
+++ b/solution.py
@@ -320,15 +320,22 @@
                     out[c * chunk : (c + 1) * chunk] = refs[(2 * p + 1 - parity) * count + c][...]
 
 
-def last_kernel(after, *refs):
-    out = refs[-1]
-    groups = [(refs[i], refs[i + 1]) for i in range(0, len(refs) - 1, 2)]
-    slots, micro, parts, lanes = groups[0][0].shape
+def rows_kernel(mine, other, after, out, token):
+    slots, micro, parts, lanes = mine.shape
     for k in range(slots):
-        total = jnp.concatenate([mine[k].astype(F32) + other[k].astype(F32) for mine, other in groups])
-        total = jnp.swapaxes(total, 0, 1)
+        total = jnp.swapaxes(mine[k].astype(F32) + other[k].astype(F32), 0, 1)
         for i in range(parts):
             out[k, :, i * lanes : (i + 1) * lanes] = total[i]
+
+
+def last_kernel(after, rows, mine, other, out):
+    slots, micro, parts, lanes = mine.shape
+    done = rows.shape[1]
+    out[:, :done] = rows[...]
+    for k in range(slots):
+        total = jnp.swapaxes(mine[k].astype(F32) + other[k].astype(F32), 0, 1)
+        for i in range(parts):
+            out[k, done : done + micro, i * lanes : (i + 1) * lanes] = total[i]
 
 
 def swaps(axes):
@@ -528,8 +535,10 @@
         late.turn()
         if segment_out is None:
             segment_out = collect()
-    ins = [last, early.mine, early.other, late.mine, late.other]
-    (total,) = call(last_kernel, "last", ins, [VMEM] * 5, [((slots, micro, rank * rank), F32)])
+    done = ((slots, 2 * chunk, rank * rank), F32)
+    (begun,) = in_turn(rows_kernel, "rows", [early.mine, early.other], [], [done])
+    ins = [last, begun, late.mine, late.other]
+    (total,) = call(last_kernel, "last", ins, [VMEM] * 4, [((slots, micro, rank * rank), F32)])
 
     return (segment_out[None], total[None])
 

time: 51.2 us -> 51.4 us (level)
  the two profiles are of different devices: /device:TPU:0 before, /device:TPU:4 now
where the time goes in v2:
time: 51.4 us; the launch traced here: 51.2 us
  starting transfers between devices  22.5 us (44%)
  waiting for transfers between devices  15.3 us (30%)
  Pallas kernels  12.6 us (25%)
  between operations  0.83 us (2%)
    ppermute x8, starting transfers between devices, exchange(): lax.ppermute(x, axis, [(i, i ^ by) for i in range(lax.axis_size(axis))])  14.5 us
    ppermute x8, waiting for transfers between devices, exchange(): lax.ppermute(x, axis, [(i, i ^ by) for i in range(lax.axis_size(axis))])  13.3 us
    pallas_call x27, Pallas kernels, call(): pl.pallas_call(kernel, out_shape=outs, in_specs=specs, out_specs=(VMEM,)...  12.6 us
    ppermute x8, starting transfers between devices, keep(): core[p].append(lax.ppermute(grad, 'pipe', swap))  4.74 us
    ppermute x4, starting transfers between devices, keep(): hops[p].append(lax.ppermute(grad, 'pipe', hop))  3.26 us
    ppermute x8, waiting for transfers between devices, keep(): core[p].append(lax.ppermute(grad, 'pipe', swap))  1.98 us
  transfers between devices with their start and end apart: 20, of which 11 were waited for; matrix products, arithmetic and copies ran while one was open for 0% of the time, Pallas kernels for 15%

profile of v2, /device:TPU:4, one launch (start us, length us, event | category | flops | bytes accessed | tf_op | source)
XLA Modules:
  0.0 51.2 jit_solution(2574768822056355738)
XLA Ops:
  0.6 3.5 %first.1 = (bf16[2,64,1024]{2,1,0:T(8,128)(2,1)S(1)}, bf16[3,128,128]{2,1,0:T(8,128)(2,1)S(1)}, f32[3,2,64,1024]{3,2,1,0:T(8,128)S(1)}, bf16[3,128,128]{2,1,0:T(...) custom-call(s32[4]{0:T(128)} %sizes_in.1, ...), custom_call_target="tpu_custom_call" | custom-call | flops 1000 | bytes 1000 | tf_op jit(solution)/shard_map/first/pallas_call | solution.py:378
  4.2 0.8 %collective-permute-start.1 = (bf16[2,64,1024]{2,1,0:T(8,128)(2,1)S(1)}, bf16[2,64,1024]{2,1,0:T(8,128)(2,1)S(1)}, u32[]{:S(2)}, u32[]{:S(2)}) collective-permute-start(bf16[2,64,1024]{2,1,0:T(8,128)(2,1)S(1)} %get-tuple-element.84.refs_0_), channel_id=1, source_target_pairs={{0,4},{4,0},{8,12},{12,8},{1,5},{5,1},{9,13},{13,9},{2,6},{6,2},{1... | collective-permute-start | bytes 786440 | tf_op jit(solution)/shard_map/ppermute | solution.py:442
  5.0 0.9 %beside.1 = (f32[3,2,64,1024]{3,2,1,0:T(8,128)S(1)}, bf16[2,3,128,128]{3,2,1,0:T(8,128)(2,1)S(1)}, f32[8,128]{1,0:T(8,128)S(1)}) custom-call(f32[8,128]{1,0:T(8,128)S(1)} %get-tuple-element.76.info.after, bf16[3,8,64,1024]{3,2,1,0:T(8,128)(2,1)S(1)} %get-tuple-element.77.acts.refs_1_, bf16[3,8,128,256]{3,2,1,0:T(8,128)(2,1)S(1)} %get-tuple-element.78.mix_act.refs_2_, ...), custom_call_target="tpu_custom_call" | custom-call | flops 3000000000 | bytes 1000 | tf_op jit(solution)/shard_map/beside/pallas_call | solution.py:378
  5.9 0.3 collective-permute-done.1.even_in
  6.1 0.7 %top.6 = (bf16[2,64,1024]{2,1,0:T(8,128)(2,1)S(1)}, bf16[3,128,128]{2,1,0:T(8,128)(2,1)S(1)}, f32[8,128]{1,0:T(8,128)S(1)}) custom-call(f32[8,128]{1,0:T(8,128)S(1)} %get-tuple-element.76.info.after, bf16[3,8,256,128]{3,2,1,0:T(8,128)(2,1)S(1)} %get-tuple-element.82.mix_grad, f32[8,128]{1,0:T(8,128)S(1)} %get-tuple-element.83.after, ...), custom_call_target="tpu_custom_call" | custom-call | flops 1000000000 | bytes 1000 | tf_op jit(solution)/shard_map/top/pallas_call | solution.py:378
  6.9 1.7 %collective-permute-start.2 = (bf16[2,64,1024]{2,1,0:T(8,128)(2,1)S(1)}, bf16[2,64,1024]{2,1,0:T(8,128)(2,1)S(1)}, u32[]{:S(2)}, u32[]{:S(2)}) collective-permute-start(bf16[2,64,1024]{2,1,0:T(8,128)(2,1)S(1)} %get-tuple-element.88.refs_1_.refs_4_), channel_id=1, source_target_pairs={{0,4},{4,0},{8,12},{12,8},{1,5},{5,1},{9,13},{13,9},{2,6},{6,2},{1... | collective-permute-start | bytes 786440 | tf_op jit(solution)/shard_map/ppermute | solution.py:442
  8.6 1.4 %collective-permute-start = (bf16[2,3,128,128]{3,2,1,0:T(8,128)(2,1)S(1)}, bf16[2,3,128,128]{3,2,1,0:T(8,128)(2,1)S(1)}, u32[]{:S(2)}, u32[]{:S(2)}) collective-permute-start(bf16[2,3,128,128]{3,2,1,0:T(8,128)(2,1)S(1)} %get-tuple-element.81.mine), channel_id=1, source_target_pairs={{0,1},{1,0},{2,3},{3,2},{4,5},{5,4},{6,7},{7,6},{8,9},{9,8},{10,11... | collective-permute-start | bytes 589832 | tf_op jit(solution)/shard_map/ppermute | solution.py:356
  10.0 1.3 %collective-permute-start.5 = (bf16[2,64,1024]{2,1,0:T(8,128)(2,1)S(1)}, bf16[2,64,1024]{2,1,0:T(8,128)(2,1)S(1)}, u32[]{:S(2)}, u32[]{:S(2)}) collective-permute-start(bf16[2,64,1024]{2,1,0:T(8,128)(2,1)S(1)} %get-tuple-element.88.refs_1_.refs_4_), channel_id=1, source_target_pairs={{8,4},{9,5},{10,6},{11,7},{24,20},{25,21},{26,22},{27,23}} | collective-permute-start | bytes 786440 | tf_op jit(solution)/shard_map/ppermute | solution.py:448
  11.3 0.0 collective-permute-done.2.even_in
  11.3 0.8 %top.7 = (bf16[2,64,1024]{2,1,0:T(8,128)(2,1)S(1)}, bf16[3,128,128]{2,1,0:T(8,128)(2,1)S(1)}, f32[8,128]{1,0:T(8,128)S(1)}) custom-call(f32[8,128]{1,0:T(8,128)S(1)} %get-tuple-element.76.info.after, bf16[3,8,256,128]{3,2,1,0:T(8,128)(2,1)S(1)} %get-tuple-element.82.mix_grad, f32[8,128]{1,0:T(8,128)S(1)} %get-tuple-element.87.after, ...), custom_call_target="tpu_custom_call" | custom-call | flops 6000000000 | bytes 1000 | tf_op jit(solution)/shard_map/top/pallas_call | solution.py:378
  12.1 0.5 %collective-permute-start.4 = (bf16[2,64,1024]{2,1,0:T(8,128)(2,1)S(1)}, bf16[2,64,1024]{2,1,0:T(8,128)(2,1)S(1)}, u32[]{:S(2)}, u32[]{:S(2)}) collective-permute-start(bf16[2,64,1024]{2,1,0:T(8,128)(2,1)S(1)} %get-tuple-element.94.refs_2_.refs_5_), channel_id=1, source_target_pairs={{0,4},{4,0},{8,12},{12,8},{1,5},{5,1},{9,13},{13,9},{2,6},{6,2},{1... | collective-permute-start | bytes 786440 | tf_op jit(solution)/shard_map/ppermute | solution.py:442
  12.6 1.3 %collective-permute-start.7 = (bf16[2,64,1024]{2,1,0:T(8,128)(2,1)S(1)}, bf16[2,64,1024]{2,1,0:T(8,128)(2,1)S(1)}, u32[]{:S(2)}, u32[]{:S(2)}) collective-permute-start(bf16[2,64,1024]{2,1,0:T(8,128)(2,1)S(1)} %get-tuple-element.94.refs_2_.refs_5_), channel_id=1, source_target_pairs={{8,4},{9,5},{10,6},{11,7},{24,20},{25,21},{26,22},{27,23}} | collective-permute-start | bytes 786440 | tf_op jit(solution)/shard_map/ppermute | solution.py:448
  13.9 0.7 %slope.1 = (f32[3,2,64,1024]{3,2,1,0:T(8,128)S(1)}, f32[8,128]{1,0:T(8,128)S(1)}) custom-call(f32[8,128]{1,0:T(8,128)S(1)} %get-tuple-element.76.info.after, bf16[3,8,64,1024]{3,2,1,0:T(8,128)(2,1)S(1)} %get-tuple-element.77.acts.refs_1_, bf16[3,8,128,256]{3,2,1,0:T(8,128)(2,1)S(1)} %get-tuple-element.78.mix_act.refs_2_, f32[8,128]{1,0:T(8,128)S(1)} %get-tuple-element.90.after), custom_call_target="tpu_custom_call" | custom-call | flops 1000000000 | bytes 1000 | tf_op jit(solution)/shard_map/slope/pallas_call | solution.py:378
  14.6 0.8 %collective-permute-done.other = bf16[2,3,128,128]{3,2,1,0:T(8,128)(2,1)S(1)} collective-permute-done((bf16[2,3,128,128]{3,2,1,0:T(8,128)(2,1)S(1)}, bf16[2,3,128,128]{3,2,1,0:T(8,128)(2,1)S(1)}, u32[]{:S(2)}, u32[]{:S(2)}) %collective-permute-start) | collective-permute-done | bytes 196640 | tf_op jit(solution)/shard_map/ppermute | solution.py:356
  15.5 2.8 %collective-permute-start.3 = (bf16[2,3,128,128]{3,2,1,0:T(8,128)(2,1)S(1)}, bf16[2,3,128,128]{3,2,1,0:T(8,128)(2,1)S(1)}, u32[]{:S(2)}, u32[]{:S(2)}) collective-permute-start(bf16[2,3,128,128]{3,2,1,0:T(8,128)(2,1)S(1)} %get-tuple-element.92.mine), channel_id=1, source_target_pairs={{0,2},{1,3},{2,0},{3,1},{4,6},{5,7},{6,4},{7,5},{8,10},{9,11},{10,... | collective-permute-start | bytes 589832 | tf_op jit(solution)/shard_map/ppermute | solution.py:356
  18.3 0.7 %top.8 = (bf16[2,64,1024]{2,1,0:T(8,128)(2,1)S(1)}, bf16[3,128,128]{2,1,0:T(8,128)(2,1)S(1)}, f32[8,128]{1,0:T(8,128)S(1)}) custom-call(f32[8,128]{1,0:T(8,128)S(1)} %get-tuple-element.76.info.after, bf16[3,8,256,128]{3,2,1,0:T(8,128)(2,1)S(1)} %get-tuple-element.82.mix_grad, f32[8,128]{1,0:T(8,128)S(1)} %get-tuple-element.93.after, ...), custom_call_target="tpu_custom_call" | custom-call | flops 6000000000 | bytes 1000 | tf_op jit(solution)/shard_map/top/pallas_call | solution.py:378
  19.0 0.6 %collective-permute-start.6 = (bf16[2,64,1024]{2,1,0:T(8,128)(2,1)S(1)}, bf16[2,64,1024]{2,1,0:T(8,128)(2,1)S(1)}, u32[]{:S(2)}, u32[]{:S(2)}) collective-permute-start(bf16[2,64,1024]{2,1,0:T(8,128)(2,1)S(1)} %get-tuple-element.98.refs_3_.refs_6_), channel_id=1, source_target_pairs={{0,4},{4,0},{8,12},{12,8},{1,5},{5,1},{9,13},{13,9},{2,6},{6,2},{1... | collective-permute-start | bytes 786440 | tf_op jit(solution)/shard_map/ppermute | solution.py:442
  19.7 0.0 collective-permute-start.10
  19.7 0.0 collective-permute-done.5.source
  19.7 0.5 collective-permute-start.8
  20.2 0.6 %collective-permute-done.6.even_in = bf16[2,64,1024]{2,1,0:T(8,128)(2,1)S(1)} collective-permute-done((bf16[2,64,1024]{2,1,0:T(8,128)(2,1)S(1)}, bf16[2,64,1024]{2,1,0:T(8,128)(2,1)S(1)}, u32[]{:S(2)}, u32[]{:S(2)}) %collective-permute-start.6) | collective-permute-done | bytes 262176 | tf_op jit(solution)/shard_map/ppermute | solution.py:442
  20.8 0.7 %top.9 = (bf16[2,64,1024]{2,1,0:T(8,128)(2,1)S(1)}, bf16[3,128,128]{2,1,0:T(8,128)(2,1)S(1)}, f32[8,128]{1,0:T(8,128)S(1)}) custom-call(f32[8,128]{1,0:T(8,128)S(1)} %get-tuple-element.76.info.after, bf16[3,8,256,128]{3,2,1,0:T(8,128)(2,1)S(1)} %get-tuple-element.82.mix_grad, f32[8,128]{1,0:T(8,128)S(1)} %get-tuple-element.97.after, ...), custom_call_target="tpu_custom_call" | custom-call | flops 6000000000 | bytes 1000 | tf_op jit(solution)/shard_map/top/pallas_call | solution.py:378
  21.6 0.2 step.9
  21.8 0.1 collective-permute-start.9
  21.9 0.7 %collective-permute-start.11 = (bf16[2,64,1024]{2,1,0:T(8,128)(2,1)S(1)}, bf16[2,64,1024]{2,1,0:T(8,128)(2,1)S(1)}, u32[]{:S(2)}, u32[]{:S(2)}) collective-permute-start(bf16[2,64,1024]{2,1,0:T(8,128)(2,1)S(1)} %get-tuple-element.117.refs_7_), channel_id=1, source_target_pairs={{0,12},{4,0},{8,4},{12,8},{1,13},{5,1},{9,5},{13,9},{2,14},{6,2},{... | collective-permute-start | bytes 786440 | tf_op jit(solution)/shard_map/ppermute | solution.py:448
  22.5 0.8 %collective-permute-done.9.source = bf16[2,64,1024]{2,1,0:T(8,128)(2,1)S(1)} collective-permute-done((bf16[2,64,1024]{2,1,0:T(8,128)(2,1)S(1)}, bf16[2,64,1024]{2,1,0:T(8,128)(2,1)S(1)}, u32[]{:S(2)}, u32[]{:S(2)}) %collective-permute-start.9) | collective-permute-done | bytes 262176 | tf_op jit(solution)/shard_map/ppermute | solution.py:442
  23.4 3.7 %collective-permute-done.3.other = bf16[2,3,128,128]{3,2,1,0:T(8,128)(2,1)S(1)} collective-permute-done((bf16[2,3,128,128]{3,2,1,0:T(8,128)(2,1)S(1)}, bf16[2,3,128,128]{3,2,1,0:T(8,128)(2,1)S(1)}, u32[]{:S(2)}, u32[]{:S(2)}) %collective-permute-start.3) | collective-permute-done | bytes 196640 | tf_op jit(solution)/shard_map/ppermute | solution.py:356
  27.1 0.1 widen.2
  27.2 0.9 %sketch.2 = (bf16[3,4,32,128]{3,2,1,0:T(8,128)(2,1)S(1)}, f32[8,128]{1,0:T(8,128)S(1)}) custom-call(f32[8,128]{1,0:T(8,128)S(1)} %get-tuple-element.76.info.after, f32[8,128]{1,0:T(8,128)S(1)} %get-tuple-element.106.after, bf16[3,128,128]{2,1,0:T(8,128)(2,1)S(1)} %get-tuple-element.107.refs_0_, bf16[3,128,128]{2,1,0:T(8,128)(2,1)S(1)} %get-tuple-element.108.refs_1_.refs_2_, ...), custom_call_target="tpu_custom_call" | custom-call | flops 2000000000 | bytes 1000 | tf_op jit(solution)/shard_map/sketch/pallas_call | solution.py:378
  28.2 0.1 collective-permute-start.12
  28.3 0.5 collective-permute-start.13
  28.8 1.2 %collective-permute-start.15 = (bf16[3,4,32,128]{3,2,1,0:T(8,128)(2,1)S(1)}, bf16[3,4,32,128]{3,2,1,0:T(8,128)(2,1)S(1)}, u32[]{:S(2)}, u32[]{:S(2)}) collective-permute-start(bf16[3,4,32,128]{3,2,1,0:T(8,128)(2,1)S(1)} %get-tuple-element.132.mine), channel_id=1, source_target_pairs={{0,1},{1,0},{2,3},{3,2},{4,5},{5,4},{6,7},{7,6},{8,9},{9,8},{10,11... | collective-permute-start | bytes 294920 | tf_op jit(solution)/shard_map/ppermute | solution.py:356
  30.0 0.2 collective-permute-done.13.source
  30.2 0.1 widen.3
  30.3 0.9 %sketch.3 = (bf16[3,4,32,128]{3,2,1,0:T(8,128)(2,1)S(1)}, f32[8,128]{1,0:T(8,128)S(1)}) custom-call(f32[8,128]{1,0:T(8,128)S(1)} %get-tuple-element.76.info.after, f32[8,128]{1,0:T(8,128)S(1)} %get-tuple-element.123.after, bf16[3,128,128]{2,1,0:T(8,128)(2,1)S(1)} %get-tuple-element.109.refs_3_.refs_0_, ...), custom_call_target="tpu_custom_call" | custom-call | flops 1000000 | bytes 1000 | tf_op jit(solution)/shard_map/sketch/pallas_call | solution.py:378
  31.2 1.6 %collective-permute-start.14 = (bf16[3,4,32,128]{3,2,1,0:T(8,128)(2,1)S(1)}, bf16[3,4,32,128]{3,2,1,0:T(8,128)(2,1)S(1)}, u32[]{:S(2)}, u32[]{:S(2)}) collective-permute-start(bf16[3,4,32,128]{3,2,1,0:T(8,128)(2,1)S(1)} %get-tuple-element.131.mine), channel_id=1, source_target_pairs={{0,16},{16,0},{1,17},{17,1},{2,18},{18,2},{3,19},{19,3},{4,20},{20... | collective-permute-start | bytes 294920 | tf_op jit(solution)/shard_map/ppermute | solution.py:356
  32.8 0.8 %collective-permute-done.15.other = bf16[3,4,32,128]{3,2,1,0:T(8,128)(2,1)S(1)} collective-permute-done((bf16[3,4,32,128]{3,2,1,0:T(8,128)(2,1)S(1)}, bf16[3,4,32,128]{3,2,1,0:T(8,128)(2,1)S(1)}, u32[]{:S(2)}, u32[]{:S(2)}) %collective-permute-start.15) | collective-permute-done | bytes 98336 | tf_op jit(solution)/shard_map/ppermute | solution.py:356
  33.6 2.6 %collective-permute-start.16 = (bf16[3,4,32,128]{3,2,1,0:T(8,128)(2,1)S(1)}, bf16[3,4,32,128]{3,2,1,0:T(8,128)(2,1)S(1)}, u32[]{:S(2)}, u32[]{:S(2)}) collective-permute-start(bf16[3,4,32,128]{3,2,1,0:T(8,128)(2,1)S(1)} %get-tuple-element.141.mine), channel_id=1, source_target_pairs={{0,2},{1,3},{2,0},{3,1},{4,6},{5,7},{6,4},{7,5},{8,10},{9,11},{10,... | collective-permute-start | bytes 294920 | tf_op jit(solution)/shard_map/ppermute | solution.py:356
  36.3 0.3 collective-permute-done.14.other
  36.6 1.6 %collective-permute-start.18 = (bf16[3,4,32,128]{3,2,1,0:T(8,128)(2,1)S(1)}, bf16[3,4,32,128]{3,2,1,0:T(8,128)(2,1)S(1)}, u32[]{:S(2)}, u32[]{:S(2)}) collective-permute-start(bf16[3,4,32,128]{3,2,1,0:T(8,128)(2,1)S(1)} %get-tuple-element.144.mine), channel_id=1, source_target_pairs={{0,1},{1,0},{2,3},{3,2},{4,5},{5,4},{6,7},{7,6},{8,9},{9,8},{10,11... | collective-permute-start | bytes 294920 | tf_op jit(solution)/shard_map/ppermute | solution.py:356
  38.1 1.0 %collect.1 = (bf16[8,64,1024]{2,1,0:T(8,128)(2,1)}, f32[8,128]{1,0:T(8,128)S(1)}) custom-call(f32[8,128]{1,0:T(8,128)S(1)} %get-tuple-element.135.after, bf16[2,64,1024]{2,1,0:T(8,128)(2,1)S(1)} %get-tuple-element.84.refs_0_, bf16[2,64,1024]{2,1,0:T(8,128)(2,1)S(1)} %get-tuple-element.88.refs_1_.refs_4_, ...), custom_call_target="tpu_custom_call" | custom-call | flops 10000000000 | bytes 1000 | tf_op jit(solution)/shard_map/collect/pallas_call | solution.py:378
  39.2 2.1 %collective-permute-done.16.other = bf16[3,4,32,128]{3,2,1,0:T(8,128)(2,1)S(1)} collective-permute-done((bf16[3,4,32,128]{3,2,1,0:T(8,128)(2,1)S(1)}, bf16[3,4,32,128]{3,2,1,0:T(8,128)(2,1)S(1)}, u32[]{:S(2)}, u32[]{:S(2)}) %collective-permute-start.16) | collective-permute-done | bytes 98336 | tf_op jit(solution)/shard_map/ppermute | solution.py:356
  41.3 1.6 %collective-permute-start.17 = (bf16[3,4,32,128]{3,2,1,0:T(8,128)(2,1)S(1)}, bf16[3,4,32,128]{3,2,1,0:T(8,128)(2,1)S(1)}, u32[]{:S(2)}, u32[]{:S(2)}) collective-permute-start(bf16[3,4,32,128]{3,2,1,0:T(8,128)(2,1)S(1)} %get-tuple-element.143.mine), channel_id=1, source_target_pairs={{0,16},{16,0},{1,17},{17,1},{2,18},{18,2},{3,19},{19,3},{4,20},{20... | collective-permute-start | bytes 294920 | tf_op jit(solution)/shard_map/ppermute | solution.py:356
  42.9 1.8 %collective-permute-start.19 = (bf16[3,4,32,128]{3,2,1,0:T(8,128)(2,1)S(1)}, bf16[3,4,32,128]{3,2,1,0:T(8,128)(2,1)S(1)}, u32[]{:S(2)}, u32[]{:S(2)}) collective-permute-start(bf16[3,4,32,128]{3,2,1,0:T(8,128)(2,1)S(1)} %get-tuple-element.149.mine), channel_id=1, source_target_pairs={{0,2},{1,3},{2,0},{3,1},{4,6},{5,7},{6,4},{7,5},{8,10},{9,11},{10,... | collective-permute-start | bytes 294920 | tf_op jit(solution)/shard_map/ppermute | solution.py:356
  44.7 1.3 %collective-permute-done.17.other = bf16[3,4,32,128]{3,2,1,0:T(8,128)(2,1)S(1)} collective-permute-done((bf16[3,4,32,128]{3,2,1,0:T(8,128)(2,1)S(1)}, bf16[3,4,32,128]{3,2,1,0:T(8,128)(2,1)S(1)}, u32[]{:S(2)}, u32[]{:S(2)}) %collective-permute-start.17) | collective-permute-done | bytes 98336 | tf_op jit(solution)/shard_map/ppermute | solution.py:356
  45.9 0.1 rows.1
  46.0 4.4 %collective-permute-done.19.other = bf16[3,4,32,128]{3,2,1,0:T(8,128)(2,1)S(1)} collective-permute-done((bf16[3,4,32,128]{3,2,1,0:T(8,128)(2,1)S(1)}, bf16[3,4,32,128]{3,2,1,0:T(8,128)(2,1)S(1)}, u32[]{:S(2)}, u32[]{:S(2)}) %collective-permute-start.19) | collective-permute-done | bytes 98336 | tf_op jit(solution)/shard_map/ppermute | solution.py:356
  50.4 0.8 %last.1 = f32[3,8,4096]{2,1,0:T(8,128)} custom-call(f32[8,128]{1,0:T(8,128)S(1)} %get-tuple-element.147.after, f32[3,4,4096]{2,1,0:T(4,128)S(1)} %get-tuple-element.148.rows, bf16[3,4,32,128]{3,2,1,0:T(8,128)(2,1)S(1)} %get-tuple-element.149.mine, bf16[3,4,32,128]{3,2,1,0:T(8,128)(2,1)S(1)} %collective-permute-done.19.other), custom_call_target="tpu_custom_call" | custom-call | flops 1000 | bytes 1000 | tf_op jit(solution)/shard_map/last/pallas_call | solution.py:378
  (19 shorter events, 0.2 us)
Async XLA Ops:
  4.2 1.9 %collective-permute-start.1 = (bf16[2,64,1024]{2,1,0:T(8,128)(2,1)S(1)}, bf16[2,64,1024]{2,1,0:T(8,128)(2,1)S(1)}, u32[]{:S(2)}, u32[]{:S(2)}) collective-permute-start(bf16[2,64,1024]{2,1,0:T(8,128)(2,1)S(1)} %get-tuple-element.84.refs_0_), channel_id=1, source_target_pairs={{0,4},{4,0},{8,12},{12,8},{1,5},{5,1},{9,13},{13,9},{2,6},{6,2},{1... | collective-permute-start | bytes 786440 | tf_op jit(solution)/shard_map/ppermute | solution.py:442
  6.9 4.4 %collective-permute-start.2 = (bf16[2,64,1024]{2,1,0:T(8,128)(2,1)S(1)}, bf16[2,64,1024]{2,1,0:T(8,128)(2,1)S(1)}, u32[]{:S(2)}, u32[]{:S(2)}) collective-permute-start(bf16[2,64,1024]{2,1,0:T(8,128)(2,1)S(1)} %get-tuple-element.88.refs_1_.refs_4_), channel_id=1, source_target_pairs={{0,4},{4,0},{8,12},{12,8},{1,5},{5,1},{9,13},{13,9},{2,6},{6,2},{1... | collective-permute-start | bytes 786440 | tf_op jit(solution)/shard_map/ppermute | solution.py:442
  8.6 6.9 %collective-permute-start = (bf16[2,3,128,128]{3,2,1,0:T(8,128)(2,1)S(1)}, bf16[2,3,128,128]{3,2,1,0:T(8,128)(2,1)S(1)}, u32[]{:S(2)}, u32[]{:S(2)}) collective-permute-start(bf16[2,3,128,128]{3,2,1,0:T(8,128)(2,1)S(1)} %get-tuple-element.81.mine), channel_id=1, source_target_pairs={{0,1},{1,0},{2,3},{3,2},{4,5},{5,4},{6,7},{7,6},{8,9},{9,8},{10,11... | collective-permute-start | bytes 589832 | tf_op jit(solution)/shard_map/ppermute | solution.py:356
  10.0 9.7 %collective-permute-start.5 = (bf16[2,64,1024]{2,1,0:T(8,128)(2,1)S(1)}, bf16[2,64,1024]{2,1,0:T(8,128)(2,1)S(1)}, u32[]{:S(2)}, u32[]{:S(2)}) collective-permute-start(bf16[2,64,1024]{2,1,0:T(8,128)(2,1)S(1)} %get-tuple-element.88.refs_1_.refs_4_), channel_id=1, source_target_pairs={{8,4},{9,5},{10,6},{11,7},{24,20},{25,21},{26,22},{27,23}} | collective-permute-start | bytes 786440 | tf_op jit(solution)/shard_map/ppermute | solution.py:448
  12.1 6.2 %collective-permute-start.4 = (bf16[2,64,1024]{2,1,0:T(8,128)(2,1)S(1)}, bf16[2,64,1024]{2,1,0:T(8,128)(2,1)S(1)}, u32[]{:S(2)}, u32[]{:S(2)}) collective-permute-start(bf16[2,64,1024]{2,1,0:T(8,128)(2,1)S(1)} %get-tuple-element.94.refs_2_.refs_5_), channel_id=1, source_target_pairs={{0,4},{4,0},{8,12},{12,8},{1,5},{5,1},{9,13},{13,9},{2,6},{6,2},{1... | collective-permute-start | bytes 786440 | tf_op jit(solution)/shard_map/ppermute | solution.py:442
  12.6 9.0 %collective-permute-start.7 = (bf16[2,64,1024]{2,1,0:T(8,128)(2,1)S(1)}, bf16[2,64,1024]{2,1,0:T(8,128)(2,1)S(1)}, u32[]{:S(2)}, u32[]{:S(2)}) collective-permute-start(bf16[2,64,1024]{2,1,0:T(8,128)(2,1)S(1)} %get-tuple-element.94.refs_2_.refs_5_), channel_id=1, source_target_pairs={{8,4},{9,5},{10,6},{11,7},{24,20},{25,21},{26,22},{27,23}} | collective-permute-start | bytes 786440 | tf_op jit(solution)/shard_map/ppermute | solution.py:448
  15.5 11.6 %collective-permute-start.3 = (bf16[2,3,128,128]{3,2,1,0:T(8,128)(2,1)S(1)}, bf16[2,3,128,128]{3,2,1,0:T(8,128)(2,1)S(1)}, u32[]{:S(2)}, u32[]{:S(2)}) collective-permute-start(bf16[2,3,128,128]{3,2,1,0:T(8,128)(2,1)S(1)} %get-tuple-element.92.mine), channel_id=1, source_target_pairs={{0,2},{1,3},{2,0},{3,1},{4,6},{5,7},{6,4},{7,5},{8,10},{9,11},{10,... | collective-permute-start | bytes 589832 | tf_op jit(solution)/shard_map/ppermute | solution.py:356
  19.0 1.8 %collective-permute-start.6 = (bf16[2,64,1024]{2,1,0:T(8,128)(2,1)S(1)}, bf16[2,64,1024]{2,1,0:T(8,128)(2,1)S(1)}, u32[]{:S(2)}, u32[]{:S(2)}) collective-permute-start(bf16[2,64,1024]{2,1,0:T(8,128)(2,1)S(1)} %get-tuple-element.98.refs_3_.refs_6_), channel_id=1, source_target_pairs={{0,4},{4,0},{8,12},{12,8},{1,5},{5,1},{9,13},{13,9},{2,6},{6,2},{1... | collective-permute-start | bytes 786440 | tf_op jit(solution)/shard_map/ppermute | solution.py:442
  19.7 8.5 %collective-permute-start.10 = (bf16[2,64,1024]{2,1,0:T(8,128)(2,1)S(1)}, bf16[2,64,1024]{2,1,0:T(8,128)(2,1)S(1)}, u32[]{:S(2)}, u32[]{:S(2)}) collective-permute-start(bf16[2,64,1024]{2,1,0:T(8,128)(2,1)S(1)} %get-tuple-element.98.refs_3_.refs_6_), channel_id=1, source_target_pairs={{0,12},{4,0},{8,4},{12,8},{1,13},{5,1},{9,5},{13,9},{2,14},{6,2},{... | collective-permute-start | bytes 786440 | tf_op jit(solution)/shard_map/ppermute | solution.py:448
  19.7 2.9 %collective-permute-start.8 = (bf16[2,64,1024]{2,1,0:T(8,128)(2,1)S(1)}, bf16[2,64,1024]{2,1,0:T(8,128)(2,1)S(1)}, u32[]{:S(2)}, u32[]{:S(2)}) collective-permute-start(bf16[2,64,1024]{2,1,0:T(8,128)(2,1)S(1)} %get-tuple-element.102.refs_8_), channel_id=1, source_target_pairs={{0,4},{4,0},{8,12},{12,8},{1,5},{5,1},{9,13},{13,9},{2,6},{6,2},{1... | collective-permute-start | bytes 786440 | tf_op jit(solution)/shard_map/ppermute | solution.py:442
  21.8 1.6 %collective-permute-start.9 = (bf16[2,64,1024]{2,1,0:T(8,128)(2,1)S(1)}, bf16[2,64,1024]{2,1,0:T(8,128)(2,1)S(1)}, u32[]{:S(2)}, u32[]{:S(2)}) collective-permute-start(bf16[2,64,1024]{2,1,0:T(8,128)(2,1)S(1)} %get-tuple-element.104.refs_9_), channel_id=1, source_target_pairs={{0,4},{4,0},{8,12},{12,8},{1,5},{5,1},{9,13},{13,9},{2,6},{6,2},{1... | collective-permute-start | bytes 786440 | tf_op jit(solution)/shard_map/ppermute | solution.py:442
  21.9 6.4 %collective-permute-start.11 = (bf16[2,64,1024]{2,1,0:T(8,128)(2,1)S(1)}, bf16[2,64,1024]{2,1,0:T(8,128)(2,1)S(1)}, u32[]{:S(2)}, u32[]{:S(2)}) collective-permute-start(bf16[2,64,1024]{2,1,0:T(8,128)(2,1)S(1)} %get-tuple-element.117.refs_7_), channel_id=1, source_target_pairs={{0,12},{4,0},{8,4},{12,8},{1,13},{5,1},{9,5},{13,9},{2,14},{6,2},{... | collective-permute-start | bytes 786440 | tf_op jit(solution)/shard_map/ppermute | solution.py:448
  28.2 1.8 %collective-permute-start.12 = (bf16[2,64,1024]{2,1,0:T(8,128)(2,1)S(1)}, bf16[2,64,1024]{2,1,0:T(8,128)(2,1)S(1)}, u32[]{:S(2)}, u32[]{:S(2)}) collective-permute-start(bf16[2,64,1024]{2,1,0:T(8,128)(2,1)S(1)} %get-tuple-element.119.refs_10_), channel_id=1, source_target_pairs={{0,4},{4,0},{8,12},{12,8},{1,5},{5,1},{9,13},{13,9},{2,6},{6,2},{1... | collective-permute-start | bytes 786440 | tf_op jit(solution)/shard_map/ppermute | solution.py:442
  28.3 1.9 %collective-permute-start.13 = (bf16[2,64,1024]{2,1,0:T(8,128)(2,1)S(1)}, bf16[2,64,1024]{2,1,0:T(8,128)(2,1)S(1)}, u32[]{:S(2)}, u32[]{:S(2)}) collective-permute-start(bf16[2,64,1024]{2,1,0:T(8,128)(2,1)S(1)} %get-tuple-element.121.refs_11_), channel_id=1, source_target_pairs={{0,4},{4,0},{8,12},{12,8},{1,5},{5,1},{9,13},{13,9},{2,6},{6,2},{1... | collective-permute-start | bytes 786440 | tf_op jit(solution)/shard_map/ppermute | solution.py:442
  28.8 4.8 %collective-permute-start.15 = (bf16[3,4,32,128]{3,2,1,0:T(8,128)(2,1)S(1)}, bf16[3,4,32,128]{3,2,1,0:T(8,128)(2,1)S(1)}, u32[]{:S(2)}, u32[]{:S(2)}) collective-permute-start(bf16[3,4,32,128]{3,2,1,0:T(8,128)(2,1)S(1)} %get-tuple-element.132.mine), channel_id=1, source_target_pairs={{0,1},{1,0},{2,3},{3,2},{4,5},{5,4},{6,7},{7,6},{8,9},{9,8},{10,11... | collective-permute-start | bytes 294920 | tf_op jit(solution)/shard_map/ppermute | solution.py:356
  31.2 5.3 %collective-permute-start.14 = (bf16[3,4,32,128]{3,2,1,0:T(8,128)(2,1)S(1)}, bf16[3,4,32,128]{3,2,1,0:T(8,128)(2,1)S(1)}, u32[]{:S(2)}, u32[]{:S(2)}) collective-permute-start(bf16[3,4,32,128]{3,2,1,0:T(8,128)(2,1)S(1)} %get-tuple-element.131.mine), channel_id=1, source_target_pairs={{0,16},{16,0},{1,17},{17,1},{2,18},{18,2},{3,19},{19,3},{4,20},{20... | collective-permute-start | bytes 294920 | tf_op jit(solution)/shard_map/ppermute | solution.py:356
  33.6 7.6 %collective-permute-start.16 = (bf16[3,4,32,128]{3,2,1,0:T(8,128)(2,1)S(1)}, bf16[3,4,32,128]{3,2,1,0:T(8,128)(2,1)S(1)}, u32[]{:S(2)}, u32[]{:S(2)}) collective-permute-start(bf16[3,4,32,128]{3,2,1,0:T(8,128)(2,1)S(1)} %get-tuple-element.141.mine), channel_id=1, source_target_pairs={{0,2},{1,3},{2,0},{3,1},{4,6},{5,7},{6,4},{7,5},{8,10},{9,11},{10,... | collective-permute-start | bytes 294920 | tf_op jit(solution)/shard_map/ppermute | solution.py:356
  36.6 6.3 %collective-permute-start.18 = (bf16[3,4,32,128]{3,2,1,0:T(8,128)(2,1)S(1)}, bf16[3,4,32,128]{3,2,1,0:T(8,128)(2,1)S(1)}, u32[]{:S(2)}, u32[]{:S(2)}) collective-permute-start(bf16[3,4,32,128]{3,2,1,0:T(8,128)(2,1)S(1)} %get-tuple-element.144.mine), channel_id=1, source_target_pairs={{0,1},{1,0},{2,3},{3,2},{4,5},{5,4},{6,7},{7,6},{8,9},{9,8},{10,11... | collective-permute-start | bytes 294920 | tf_op jit(solution)/shard_map/ppermute | solution.py:356
  41.3 4.7 %collective-permute-start.17 = (bf16[3,4,32,128]{3,2,1,0:T(8,128)(2,1)S(1)}, bf16[3,4,32,128]{3,2,1,0:T(8,128)(2,1)S(1)}, u32[]{:S(2)}, u32[]{:S(2)}) collective-permute-start(bf16[3,4,32,128]{3,2,1,0:T(8,128)(2,1)S(1)} %get-tuple-element.143.mine), channel_id=1, source_target_pairs={{0,16},{16,0},{1,17},{17,1},{2,18},{18,2},{3,19},{19,3},{4,20},{20... | collective-permute-start | bytes 294920 | tf_op jit(solution)/shard_map/ppermute | solution.py:356
  42.9 7.5 %collective-permute-start.19 = (bf16[3,4,32,128]{3,2,1,0:T(8,128)(2,1)S(1)}, bf16[3,4,32,128]{3,2,1,0:T(8,128)(2,1)S(1)}, u32[]{:S(2)}, u32[]{:S(2)}) collective-permute-start(bf16[3,4,32,128]{3,2,1,0:T(8,128)(2,1)S(1)} %get-tuple-element.149.mine), channel_id=1, source_target_pairs={{0,2},{1,3},{2,0},{3,1},{4,6},{5,7},{6,4},{7,5},{8,10},{9,11},{10,... | collective-permute-start | bytes 294920 | tf_op jit(solution)/shard_map/ppermute | solution.py:356
